TPU v7x, 32 devices: a whole 2x2x4 slice. The times are simulated.
32 devices in a mesh: wide: 8 (over z, x), narrow: 4 (over y, core).
Axes of the slice: x: 2, y: 2, z: 4, core: 2. Of those that a mesh axis runs over, the one named last changes fastest.
Arguments:
- tokens: bfloat16 [64, 256, 1024], P('wide'), may hold values from -6 to 6
- frame_counts: int32 [4], replicated, may hold values from 4 to 16, as said below
- actions: int32 [64], P('wide'), may hold values from 0 to 7
- action_table: bfloat16 [8, 1024], replicated, may hold values from -3 to 3
- norm_gains: float32 [3, 1024], replicated, may hold values from 0.25 to 1.75
- spatial_project: bfloat16 [1024, 3, 1024], P(None, None, 'narrow'), may hold values from -0.1875 to 0.1875
- spatial_merge: bfloat16 [1024, 1024], P('narrow'), may hold values from -0.75 to 0.75
- temporal_project: bfloat16 [1024, 3, 1024], P(None, None, 'narrow'), may hold values from -0.1875 to 0.1875
- temporal_merge: bfloat16 [1024, 1024], P('narrow'), may hold values from -0.375 to 0.375
- expand_weight: bfloat16 [1024, 4096], P(None, 'narrow'), may hold values from -0.1875 to 0.1875
- reduce_weight: bfloat16 [4096, 1024], P('narrow'), may hold values from -0.09375 to 0.09375
- grad_out: bfloat16 [64, 256, 1024], P('wide'), may hold values from -6 to 6
Outputs:
- output: bfloat16 [64, 256, 1024], P('wide')
- grad_tokens: float32 [64, 256, 1024], P('wide')
- norm_gains_grad: float32 [3, 1024], P(None, 'wide')
- action_table_grad: float32 [8, 1024], P(None, 'wide')
- spatial_project_grad: float32 [1024, 3, 1024], P('wide', None, 'narrow')
- spatial_merge_grad: float32 [1024, 1024], P('narrow', 'wide')
- temporal_project_grad: float32 [1024, 3, 1024], P('wide', None, 'narrow')
- temporal_merge_grad: float32 [1024, 1024], P('narrow', 'wide')
- expand_weight_grad: float32 [1024, 4096], P('wide', 'narrow')
- reduce_weight_grad: float32 [4096, 1024], P('narrow', 'wide')
Inputs may be any that keep to these rules, and one draw needn't show every extreme that they name: `frame_counts`: every clip has its real frames in its first slots; in every draw one clip has 16.
All inputs are finite; a program needn't handle non-finite values.
Results may differ from a plain program's by a relative error of at most 0.033.
Values may be sent and summed in bfloat16 or wider, within the bound.
A program may use at most 192 MiB of HBM per device.

v0:
```python
import jax
import jax.numpy as jnp
from jax import lax
from jax.sharding import PartitionSpec as P

HD = 64
FRAMES = 16


EPSILON = 1e-06
NEGATIVE = -1e30
HIGHEST = lax.Precision.HIGHEST
SPATIAL_FORMS = ("fqhd,fkhd->fhqk", "fhqk,fkhd->fqhd", "fhqk,fqhd->fkhd")
TEMPORAL_FORMS = ("cqphd,ckphd->cphqk", "cphqk,ckphd->cqphd", "cphqk,cqphd->ckphd")


def normalize(value, gain):
    return value * lax.rsqrt(jnp.mean(value * value, axis=-1, keepdims=True) + EPSILON) * gain


def norm_back(value, gain, incoming):
    _, pullback = jax.vjp(normalize, value, gain)
    return pullback(incoming)


def split_heads(packed, heads_dev):
    shaped = packed.reshape(packed.shape[:-1] + (heads_dev, HD))
    return (shaped[..., 0, :, :], shaped[..., 1, :, :], shaped[..., 2, :, :])


def attend(queries, key_rows, value_rows, forms, allowed):
    score_form, out_form, key_form = forms
    scores = jnp.einsum(score_form, queries, key_rows, preferred_element_type=jnp.float32) * HD ** (
        -0.5
    )
    scores = jnp.where(allowed, scores, NEGATIVE)
    highest = jnp.max(scores, axis=-1, keepdims=True)
    log_total = jnp.log(jnp.sum(jnp.exp(scores - highest), axis=-1, keepdims=True)) + highest
    shares = jnp.exp(scores - log_total).astype(jnp.bfloat16)
    mixed = jnp.einsum(out_form, shares, value_rows, preferred_element_type=jnp.float32).astype(
        jnp.bfloat16
    )
    return (mixed, log_total)


def attend_back(queries, key_rows, value_rows, log_total, grad_mixed, forms, allowed):
    score_form, out_form, key_form = forms
    factor = HD ** (-0.5)
    scores = jnp.einsum(score_form, queries, key_rows, preferred_element_type=jnp.float32) * factor
    scores = jnp.where(allowed, scores, NEGATIVE)
    chances = jnp.exp(scores - log_total)
    grad_values = jnp.einsum(
        key_form, chances.astype(jnp.bfloat16), grad_mixed, preferred_element_type=jnp.float32
    )
    grad_chances = jnp.einsum(
        score_form, grad_mixed, value_rows, preferred_element_type=jnp.float32
    )
    grad_scores = (
        chances * (grad_chances - jnp.sum(grad_chances * chances, axis=-1, keepdims=True))
    ).astype(jnp.bfloat16)
    grad_queries = (
        jnp.einsum(out_form, grad_scores, key_rows, preferred_element_type=jnp.float32) * factor
    )
    grad_keys = (
        jnp.einsum(key_form, grad_scores, queries, preferred_element_type=jnp.float32) * factor
    )
    return jnp.stack([grad_queries, grad_keys, grad_values], axis=-3).astype(jnp.bfloat16)


def body(
    tokens,
    frame_counts,
    actions,
    action_table,
    norm_gains,
    spatial_project,
    spatial_merge,
    temporal_project,
    temporal_merge,
    expand_weight,
    reduce_weight,
    grad_out,
):
    frames_dev, tokens_frame, width = tokens.shape
    local = spatial_merge.shape[0]
    heads_dev = local // HD

    def summed(term):
        return lax.psum(term.astype(jnp.bfloat16), "narrow").astype(jnp.float32)

    frame_ids = lax.axis_index("wide") * frames_dev + jnp.arange(frames_dev, dtype=jnp.int32)
    clip_ids = frame_ids // FRAMES
    clip_places = jnp.arange(frame_counts.shape[0], dtype=jnp.int32)
    clip_count = jnp.sum(
        jnp.where(clip_ids[:, None] == clip_places[None, :], frame_counts[None, :], 0), axis=1
    )
    keep_mask = (frame_ids % FRAMES < clip_count).astype(jnp.float32)[:, None, None]
    choose = (
        actions[:, None] == jnp.arange(action_table.shape[0], dtype=jnp.int32)[None, :]
    ).astype(jnp.bfloat16)
    extra = jnp.dot(choose, action_table, preferred_element_type=jnp.float32)
    start = tokens.astype(jnp.float32) + extra[:, None, :]
    normed1 = normalize(start, norm_gains[0]).astype(jnp.bfloat16)
    project1 = jnp.einsum(
        "fsd,dce->fsce", normed1, spatial_project, preferred_element_type=jnp.float32
    ).astype(jnp.bfloat16)
    heads1 = split_heads(project1, heads_dev)
    mixed1, total1 = attend(heads1[0], heads1[1], heads1[2], SPATIAL_FORMS, True)
    mixed1 = mixed1.reshape(frames_dev, tokens_frame, local)
    branch1 = summed(
        jnp.einsum("fse,ed->fsd", mixed1, spatial_merge, preferred_element_type=jnp.float32)
    )
    hidden1 = start + keep_mask * branch1
    normed2 = normalize(hidden1, norm_gains[1]).astype(jnp.bfloat16)
    normed_place = lax.all_to_all(normed2, "wide", split_axis=1, concat_axis=0, tiled=True)
    project2 = jnp.einsum(
        "fsd,dce->fsce", normed_place, temporal_project, preferred_element_type=jnp.float32
    ).astype(jnp.bfloat16)
    all_frames, positions = (project2.shape[0], project2.shape[1])
    clips = all_frames // FRAMES
    steps_all = jnp.arange(FRAMES, dtype=jnp.int32)
    allowed = steps_all[None, :] <= steps_all[:, None]
    heads2 = split_heads(project2.reshape(clips, FRAMES, positions, 3, local), heads_dev)
    mixed2, total2 = attend(heads2[0], heads2[1], heads2[2], TEMPORAL_FORMS, allowed)
    mixed2 = mixed2.reshape(all_frames, positions, local)
    mixed2_frames = lax.all_to_all(mixed2, "wide", split_axis=0, concat_axis=1, tiled=True)
    branch2 = summed(
        jnp.einsum("fse,ed->fsd", mixed2_frames, temporal_merge, preferred_element_type=jnp.float32)
    )
    hidden2 = hidden1 + keep_mask * branch2
    normed3 = normalize(hidden2, norm_gains[2]).astype(jnp.bfloat16)
    inner = jnp.einsum("fsd,de->fse", normed3, expand_weight, preferred_element_type=jnp.float32)
    active = jax.nn.gelu(inner).astype(jnp.bfloat16)
    branch3 = summed(
        jnp.einsum("fse,ed->fsd", active, reduce_weight, preferred_element_type=jnp.float32)
    )
    result = (hidden2 + keep_mask * branch3).astype(jnp.bfloat16)
    grad_result = grad_out.astype(jnp.float32)
    grad_branch3 = (keep_mask * grad_result).astype(jnp.bfloat16)
    reduce_grad = jnp.einsum(
        "fse,fsd->ed", active, grad_branch3, preferred_element_type=jnp.float32
    )
    grad_active = jnp.einsum(
        "fsd,ed->fse", grad_branch3, reduce_weight, preferred_element_type=jnp.float32
    )
    _, gelu_pull = jax.vjp(jax.nn.gelu, inner)
    grad_inner = gelu_pull(grad_active)[0].astype(jnp.bfloat16)
    expand_grad = jnp.einsum("fsd,fse->de", normed3, grad_inner, preferred_element_type=jnp.float32)
    grad_normed3 = summed(
        jnp.einsum("fse,de->fsd", grad_inner, expand_weight, preferred_element_type=jnp.float32)
    )
    back_three, gain_three = norm_back(hidden2, norm_gains[2], grad_normed3)
    grad_hidden2 = grad_result + back_three
    grad_branch2 = (keep_mask * grad_hidden2).astype(jnp.bfloat16)
    temporal_merge_grad = jnp.einsum(
        "fse,fsd->ed", mixed2_frames, grad_branch2, preferred_element_type=jnp.float32
    )
    grad_mixed2 = jnp.einsum(
        "fsd,ed->fse", grad_branch2, temporal_merge, preferred_element_type=jnp.float32
    ).astype(jnp.bfloat16)
    grad_mixed2_place = lax.all_to_all(grad_mixed2, "wide", split_axis=1, concat_axis=0, tiled=True)
    grad_mixed2_place = grad_mixed2_place.reshape(clips, FRAMES, positions, heads_dev, HD)
    grad_project2 = attend_back(
        heads2[0], heads2[1], heads2[2], total2, grad_mixed2_place, TEMPORAL_FORMS, allowed
    )
    grad_project2 = grad_project2.reshape(all_frames, positions, 3, local)
    temporal_project_grad = jnp.einsum(
        "fsd,fsce->dce", normed_place, grad_project2, preferred_element_type=jnp.float32
    )
    partial_place = jnp.einsum(
        "fsce,dce->fsd", grad_project2, temporal_project, preferred_element_type=jnp.float32
    )
    partial_two = lax.all_to_all(
        partial_place.astype(jnp.bfloat16), "wide", split_axis=0, concat_axis=1, tiled=True
    ).astype(partial_place.dtype)
    grad_normed2 = summed(partial_two)
    back_two, gain_two = norm_back(hidden1, norm_gains[1], grad_normed2)
    grad_hidden1 = grad_hidden2 + back_two
    grad_branch1 = (keep_mask * grad_hidden1).astype(jnp.bfloat16)
    spatial_merge_grad = jnp.einsum(
        "fse,fsd->ed", mixed1, grad_branch1, preferred_element_type=jnp.float32
    )
    grad_mixed1 = jnp.einsum(
        "fsd,ed->fse", grad_branch1, spatial_merge, preferred_element_type=jnp.float32
    ).astype(jnp.bfloat16)
    grad_mixed1 = grad_mixed1.reshape(frames_dev, tokens_frame, heads_dev, HD)
    grad_project1 = attend_back(
        heads1[0], heads1[1], heads1[2], total1, grad_mixed1, SPATIAL_FORMS, True
    )
    grad_project1 = grad_project1.reshape(frames_dev, tokens_frame, 3, local)
    spatial_project_grad = jnp.einsum(
        "fsd,fsce->dce", normed1, grad_project1, preferred_element_type=jnp.float32
    )
    grad_normed1 = summed(
        jnp.einsum(
            "fsce,dce->fsd", grad_project1, spatial_project, preferred_element_type=jnp.float32
        )
    )
    back_one, gain_one = norm_back(start, norm_gains[0], grad_normed1)
    grad_tokens_own = grad_hidden1 + back_one
    frame_totals = jnp.sum(grad_tokens_own, axis=1)
    table_grad = jnp.dot(choose.astype(jnp.float32).T, frame_totals, precision=HIGHEST)
    gains_grad = jnp.stack([gain_one, gain_two, gain_three])
    reduced = (
        lax.psum_scatter(
            gains_grad.astype(jnp.bfloat16), "wide", scatter_dimension=1, tiled=True
        ).astype(jnp.float32),
        lax.psum_scatter(
            table_grad.astype(jnp.bfloat16), "wide", scatter_dimension=1, tiled=True
        ).astype(jnp.float32),
        lax.psum_scatter(
            spatial_project_grad.astype(jnp.bfloat16), "wide", scatter_dimension=0, tiled=True
        ).astype(jnp.float32),
        lax.psum_scatter(
            spatial_merge_grad.astype(jnp.bfloat16), "wide", scatter_dimension=1, tiled=True
        ).astype(jnp.float32),
        lax.psum_scatter(
            temporal_project_grad.astype(jnp.bfloat16), "wide", scatter_dimension=0, tiled=True
        ).astype(jnp.float32),
        lax.psum_scatter(
            temporal_merge_grad.astype(jnp.bfloat16), "wide", scatter_dimension=1, tiled=True
        ).astype(jnp.float32),
        lax.psum_scatter(
            expand_grad.astype(jnp.bfloat16), "wide", scatter_dimension=0, tiled=True
        ).astype(jnp.float32),
        lax.psum_scatter(
            reduce_grad.astype(jnp.bfloat16), "wide", scatter_dimension=1, tiled=True
        ).astype(jnp.float32),
    )
    gains_out, table_out = (reduced[0], reduced[1])
    return (
        result,
        grad_tokens_own,
        gains_out,
        table_out,
        reduced[2],
        reduced[3],
        reduced[4],
        reduced[5],
        reduced[6],
        reduced[7],
    )


def solution(mesh):
    return jax.shard_map(
        body,
        mesh=mesh,
        in_specs=(
            P("wide", None, None),
            P(),
            P("wide"),
            P(),
            P(),
            P(None, None, "narrow"),
            P("narrow", None),
            P(None, None, "narrow"),
            P("narrow", None),
            P(None, "narrow"),
            P("narrow", None),
            P("wide", None, None),
        ),
        out_specs=(
            P("wide", None, None),
            P("wide", None, None),
            P(None, "wide"),
            P(None, "wide"),
            P("wide", None, "narrow"),
            P("narrow", "wide"),
            P("wide", None, "narrow"),
            P("narrow", "wide"),
            P("wide", "narrow"),
            P("narrow", "wide"),
        ),
        check_vma=False,
    )
```

profile of v0, /device:TPU:0, one launch (start us, length us, event | category | flops | bytes accessed | tf_op | source)
XLA Modules:
  0.0 1487.1 jit_solution(12810123167364047922)
XLA Ops:
  9.5 3.3 multiply_reduce_fusion.3
  13.4 5.5 convolution_convert_fusion.5
  26.1 3.3 convolution_convert_fusion.3
  29.6 88.2 %all-reduce.7.cloned.1.call-done = bf16[8,256,1024]{2,1,0:T(8,128)(2,1)} async-done(((bf16[8,256,1024]{2,1,0:T(8,128)(2,1)}), bf16[8,256,1024]{2,1,0:T(8,128)(2,1)}) %all-reduce.7.cloned.1.call-update) | async-done | bytes 4194320 | tf_op jit(solution)/shard_map/psum | solution.py:89
  117.8 5.6 multiply_reduce_fusion.2
  126.4 4.3 copy.129
  130.8 5.5 all-to-all-start
  136.3 93.1 %all-to-all-done = bf16[8,256,1024]{2,0,1:T(8,128)(2,1)} async-done(((bf16[8,256,1024]{2,0,1:T(8,128)(2,1)}), bf16[8,256,1024]{2,0,1:T(8,128)(2,1)}, u32[]{:S(2)}, u32[]{:S(2)}) %all-to-all-start) | async-done | bytes 4194336 | tf_op jit(solution)/shard_map/all_to_all | solution.py:115
  229.4 4.8 copy.130
  236.2 4.8 convolution_convert_fusion.4
  241.0 10.2 reshape_reshape.3
  251.1 4.7 fusion.72
  255.8 3.4 fusion.25
  263.2 2.5 copy.135
  265.7 3.9 reshape.182
  269.6 29.5 %all_to_all.69 = bf16[64,32,256]{2,1,0:T(8,128)(2,1)S(1)} all-to-all(bf16[64,32,256]{2,1,0:T(8,128)(2,1)S(1)} %reshape.182), channel_id=1, replica_groups=mesh['wide'=8,'narrow'=4] {'wide'}, dimensions={0} | all-to-all | bytes 2097152 | tf_op jit(solution)/shard_map/all_to_all | solution.py:126
  299.2 3.3 convolution_convert_fusion.2
  302.5 84.2 %all-reduce.9.cloned.1.call-done = bf16[8,256,1024]{2,1,0:T(8,128)(2,1)} async-done(((bf16[8,256,1024]{2,1,0:T(8,128)(2,1)}), bf16[8,256,1024]{2,1,0:T(8,128)(2,1)}) %all-reduce.9.cloned.1.call-update) | async-done | bytes 4194320 | tf_op jit(solution)/shard_map/psum | solution.py:89
  386.7 6.1 multiply_reduce_fusion.1
  392.8 3.2 copy-done.7
  396.1 4.7 fusion.30
  400.8 9.6 fusion.19
  412.3 6.2 convolution_convert_fusion
  418.7 85.7 %all-reduce.11.cloned.1.call-done = bf16[8,256,1024]{2,1,0:T(8,128)(2,1)} async-done(((bf16[8,256,1024]{2,1,0:T(8,128)(2,1)}), bf16[8,256,1024]{2,1,0:T(8,128)(2,1)}) %all-reduce.11.cloned.1.call-update) | async-done | bytes 4194320 | tf_op jit(solution)/shard_map/psum | solution.py:89
  504.4 6.9 fusion.10
  511.5 5.0 multiply_convert_fusion.2
  518.5 31.0 %all_to_all.70 = bf16[8,256,256]{2,0,1:T(8,128)(2,1)S(1)} all-to-all(bf16[8,256,256]{2,0,1:T(8,128)(2,1)S(1)} %copy.137), channel_id=1, replica_groups=mesh['wide'=8,'narrow'=4] {'wide'}, dimensions={1} | all-to-all | bytes 2097152 | tf_op jit(solution)/shard_map/all_to_all | solution.py:161
  551.6 5.0 convert_bitcast_fusion
  556.9 3.8 multiply_reduce_fusion.5
  562.3 2.9 fusion.41
  565.2 2.7 fusion.40
  569.1 2.5 stack.42
  571.6 4.2 copy.141
  575.9 4.3 stack.40
  580.2 2.5 copy.142
  582.7 3.5 stack.41
  586.2 5.9 bitcast_convert_fusion.1
  592.1 96.4 %all_to_all.71 = bf16[64,32,1024]{2,1,0:T(8,128)(2,1)S(1)} all-to-all(bf16[64,32,1024]{2,1,0:T(8,128)(2,1)S(1)} %bitcast_convert_fusion.1), channel_id=1, replica_groups=mesh['wide'=8,'narrow'=4] {'wide'}, dimensions={0} | all-to-all | bytes 8388608 | tf_op jit(solution)/shard_map/all_to_all | solution.py:173
  691.0 3.5 fusion.47
  695.8 10.9 bitcast_convert_fusion.2
  706.6 2.6 copy.189
  709.3 11.0 bitcast_convert_fusion.3
  720.5 6.8 bitcast_convert_fusion.4
  727.8 47.2 %all-reduce.13.cloned.1.call-done = bf16[8,256,1024]{2,1,0:T(8,128)(2,1)} async-done(((bf16[8,256,1024]{2,1,0:T(8,128)(2,1)}), bf16[8,256,1024]{2,1,0:T(8,128)(2,1)}) %all-reduce.13.cloned.1.call-update) | async-done | bytes 4194320 | tf_op jit(solution)/shard_map/psum | solution.py:89
  775.0 9.3 fusion.11
  784.4 9.1 fusion.20
  793.5 3.3 copy-done.8
  799.1 4.9 convolution_convert_fusion.7
  804.1 5.4 multiply_reduce_fusion
  815.6 3.4 multiply_convert_fusion.11
  822.2 7.8 bitcast_convert_fusion.5
  830.1 11.7 convolution_convert_fusion.1
  841.8 5.0 bitcast_convert_fusion
  849.1 62.1 %reduce-scatter.33.cloned.1.call-done = bf16[128,1024]{1,0:T(8,128)(2,1)} async-done(((bf16[1024,1024]{1,0:T(8,128)(2,1)}), bf16[128,1024]{1,0:T(8,128)(2,1)}) %reduce-scatter.33.cloned.1.call-update) | async-done | bytes 262160
  913.2 68.8 %reduce-scatter.23.cloned.1.call-done = bf16[128,1024]{1,0:T(8,128)(2,1)} async-done(((bf16[1024,1024]{1,0:T(8,128)(2,1)}), bf16[128,1024]{1,0:T(8,128)(2,1)}) %reduce-scatter.23.cloned.1.call-update) | async-done | bytes 262160 | tf_op jit(solution)/shard_map/reduce_scatter | solution.py:223
  983.8 66.6 %reduce-scatter.21.cloned.1.call-done = bf16[128,3,256]{2,0,1:T(8,128)(2,1)} async-done(((bf16[1024,3,256]{2,0,1:T(8,128)(2,1)}), bf16[128,3,256]{2,0,1:T(8,128)(2,1)}) %reduce-scatter.21.cloned.1.call-update) | async-done | bytes 196624 | tf_op jit(solution)/shard_map/reduce_scatter | solution.py:217
  1052.1 62.6 %reduce-scatter.29.cloned.1.call-done = bf16[128,256]{1,0:T(8,128)(2,1)} async-done(((bf16[1024,256]{1,0:T(8,128)(2,1)}), bf16[128,256]{1,0:T(8,128)(2,1)}) %reduce-scatter.29.cloned.1.call-update) | async-done | bytes 65552
  1116.3 66.6 %reduce-scatter.19.cloned.1.call-done = bf16[128,3,256]{2,0,1:T(8,128)(2,1)} async-done(((bf16[1024,3,256]{2,0,1:T(8,128)(2,1)}), bf16[128,3,256]{2,0,1:T(8,128)(2,1)}) %reduce-scatter.19.cloned.1.call-update) | async-done | bytes 196624 | tf_op jit(solution)/shard_map/reduce_scatter | solution.py:211
  1184.6 153.7 %all-reduce.15.cloned.1.call-done = (bf16[8,256,1024]{2,1,0:T(8,128)(2,1)}, bf16[8,256,1024]{2,1,0:T(8,128)(2,1)}) async-done(((bf16[8,256,1024]{2,1,0:T(8,128)(2,1)}, bf16[8,256,1024]{2,1,0:T(8,128)(2,1)}), (bf16[8,256,1024]{2,1,0:T(8,128)(2,1)}, bf16[8,256,1024]{2,1,0:T(8,128)(2,1)})) %all-reduce.15.cloned.1.call-update) | async-done | bytes 8388624 | tf_op jit(solution)/shard_map/psum | solution.py:89
  1338.3 7.0 fusion.12
  1345.4 7.4 fusion.70
  1355.0 8.4 add_convert_fusion
  1363.3 51.9 %reduce-scatter.25.cloned.1.call-done = bf16[128,3]{1,0:T(8,128)(2,1)} async-done(((bf16[1024,3]{1,0:T(8,128)(2,1)}), bf16[128,3]{1,0:T(8,128)(2,1)}) %reduce-scatter.25.cloned.1.call-update) | async-done | bytes 784
  1416.7 62.2 %reduce-scatter.27.cloned.1.call-done = bf16[128,8]{1,0:T(8,128)(2,1)} async-done(((bf16[1024,8]{1,0:T(8,128)(2,1)}), bf16[128,8]{1,0:T(8,128)(2,1)}) %reduce-scatter.27.cloned.1.call-update) | async-done | bytes 2064
  (221 shorter events, 60.6 us)
Async XLA Ops:
  7.2 388.9 %copy-start = (bf16[1024,1024]{1,0:T(8,128)(2,1)S(1)}, bf16[1024,1024]{1,0:T(8,128)(2,1)}, u32[]{:S(2)}) copy-start(bf16[1024,1024]{1,0:T(8,128)(2,1)} %param.21) | copy-start | bytes 6291460
  7.2 110.6 %all-reduce.7.cloned.1.call-start = ((), (), s32[]{:S(2)}) async-start(), calls=%async_computation.12 | async-start | bytes 8388608 | tf_op jit(solution)/shard_map/psum | solution.py:89
  7.2 6.2 copy-start.3
  8.2 10.8 copy-start.57
  8.2 115.8 %copy-start.55 = (f32[1,1024]{1,0:T(1,128)}, f32[1,1024]{1,0:T(1,128)S(1)}, u32[]{:S(2)}) copy-start(f32[1,1024]{1,0:T(1,128)S(1)} %get-tuple-element.27) | copy-start | bytes 12292
  12.8 6.1 copy-start.53
  26.1 3.3 copy-start.63
  117.8 6.2 copy-start.4
  117.8 6.2 copy-start.9
  130.8 98.6 %all-to-all-start = ((bf16[8,256,1024]{2,0,1:T(8,128)(2,1)}), bf16[8,256,1024]{2,0,1:T(8,128)(2,1)}, u32[]{:S(2)}, u32[]{:S(2)}) async-start(bf16[8,256,1024]{2,0,1:T(8,128)(2,1)} %copy.129), calls=%async_computation | async-start | bytes 8388608 | tf_op jit(solution)/shard_map/all_to_all | solution.py:115
  136.3 250.4 %all-reduce.9.cloned.1.call-start = ((), (), s32[]{:S(2)}) async-start(), calls=%async_computation.13 | async-start | bytes 8388608 | tf_op jit(solution)/shard_map/psum | solution.py:89
  229.4 6.8 copy-start.61
  255.8 3.5 copy-start.26
  255.8 3.5 copy-start.28
  255.8 5.3 copy-start.16
  259.3 3.9 copy-start.11
  269.6 29.6 %copy-start.45 = (bf16[256,1024]{1,0:T(8,128)(2,1)S(1)}, bf16[256,1024]{1,0:T(8,128)(2,1)}, u32[]{:S(2)}) copy-start(bf16[256,1024]{1,0:T(8,128)(2,1)} %param.20) | copy-start | bytes 1572868
  302.5 201.9 %all-reduce.11.cloned.1.call-start = ((), (), s32[]{:S(2)}) async-start(), calls=%async_computation.14 | async-start | bytes 8388608 | tf_op jit(solution)/shard_map/psum | solution.py:89
  392.8 3.3 copy-start.7
  396.1 4.7 copy-start.19
  396.1 4.7 copy-start.60
  400.8 9.6 copy-start.65
  418.6 356.3 %all-reduce.13.cloned.1.call-start = ((), (), s32[]{:S(2)}) async-start(), calls=%async_computation.15 | async-start | bytes 8388608 | tf_op jit(solution)/shard_map/psum | solution.py:89
  504.4 7.0 copy-start.14
  504.4 7.1 copy-start.20
  511.5 5.0 copy-start.46
  551.5 5.0 copy-start.12
  551.5 5.0 copy-start.17
  551.5 5.3 copy-start.30
  571.6 8.6 copy-start.25
  586.2 5.9 copy-start.37
  691.0 156.5 %reduce-scatter.31.cloned.1.call-start = ((), (), s32[]{:S(2)}) async-start(), calls=%async_computation.22 | async-start | bytes 589824
  695.5 215.7 %reduce-scatter.33.cloned.1.call-start = ((), (), s32[]{:S(2)}) async-start(), calls=%async_computation.23 | async-start | bytes 2359296
  709.2 11.2 copy-start.35
  709.2 11.2 copy-start.36
  709.3 11.2 copy-start.38
  709.3 272.7 %reduce-scatter.23.cloned.1.call-start = ((), (), s32[]{:S(2)}) async-start(), calls=%async_computation.18 | async-start | bytes 2359296 | tf_op jit(solution)/shard_map/reduce_scatter | solution.py:223
  720.3 54.6 %copy-start.48 = (f32[8,256]{1,0:T(8,128)S(1)}, f32[8,256]{1,0:T(8,128)}, u32[]{:S(2)}) copy-start(f32[8,256]{1,0:T(8,128)} %copy-done.47) | copy-start | bytes 24580
  720.4 54.6 %copy-start.56 = (f32[1,1024]{1,0:T(1,128)S(1)}, f32[1,1024]{1,0:T(1,128)}, u32[]{:S(2)}) copy-start(f32[1,1024]{1,0:T(1,128)} %copy-done.55) | copy-start | bytes 12292
  720.4 330.0 %reduce-scatter.21.cloned.1.call-start = ((), (), s32[]{:S(2)}) async-start(), calls=%async_computation.17 | async-start | bytes 1769472 | tf_op jit(solution)/shard_map/reduce_scatter | solution.py:217
  727.3 57.0 %copy-start.52 = (f32[8,256]{1,0:T(8,128)S(1)}, f32[8,256]{1,0:T(8,128)}, u32[]{:S(2)}) copy-start(f32[8,256]{1,0:T(8,128)} %copy-done.51) | copy-start | bytes 24580
  727.3 387.4 %reduce-scatter.29.cloned.1.call-start = ((), (), s32[]{:S(2)}) async-start(), calls=%async_computation.21 | async-start | bytes 589824
  774.9 9.4 copy-start.5
  775.0 9.4 copy-start.10
  775.0 9.4 copy-start.15
  784.4 12.4 copy-start.24
  793.5 3.3 copy-start.8
  799.1 4.9 copy-start.22
  799.1 5.0 copy-start.44
  804.1 5.4 slice-start
  804.1 6.0 slice-start.1
  815.4 367.6 %reduce-scatter.19.cloned.1.call-start = ((), (), s32[]{:S(2)}) async-start(), calls=%async_computation.16 | async-start | bytes 1769472 | tf_op jit(solution)/shard_map/reduce_scatter | solution.py:211
  822.2 7.8 copy-start.41
  830.0 11.8 copy-start.40
  830.0 11.8 copy-start.42
  830.0 508.3 %all-reduce.15.cloned.1.call-start = ((), (), s32[]{:S(2)}) async-start(), calls=%async_computation.24 | async-start | bytes 16777216 | tf_op jit(solution)/shard_map/psum | solution.py:89
  830.1 11.7 copy-start.62
  846.8 568.4 %reduce-scatter.25.cloned.1.call-start = ((), (), s32[]{:S(2)}) async-start(), calls=%async_computation.19 | async-start | bytes 294912
  1338.3 7.0 copy-start.50
  1338.3 7.0 copy-start.6
  1338.3 7.1 copy-start.18
  1345.4 8.4 copy-start.64
  1353.7 125.2 %reduce-scatter.27.cloned.1.call-start = ((), (), s32[]{:S(2)}) async-start(), calls=%async_computation.20 | async-start | bytes 294912
  1355.0 125.4 %copy-start.1 = (bf16[1024,1024]{1,0:T(8,128)(2,1)S(1)}, bf16[1024,1024]{1,0:T(8,128)(2,1)}, u32[]{:S(2)}) copy-start(bf16[1024,1024]{1,0:T(8,128)(2,1)} %param.21) | copy-start | bytes 6291460
  (19 other events, 39.5 us)
Sparse Core Ops, SparseCore 0:
  29.6 88.1 all-reduce.6
  302.6 84.0 all-reduce.8
  418.7 85.6 all-reduce.10
  691.1 83.7 all-reduce.12
  778.7 62.0 reduce-scatter.30
  844.6 66.6 reduce-scatter.32
  915.2 66.7 reduce-scatter.22
  985.8 64.5 reduce-scatter.20
  1053.8 60.9 reduce-scatter.28
  1118.4 64.4 reduce-scatter.18
  1186.1 152.2 all-reduce.14
  1353.9 61.3 reduce-scatter.24
  1418.6 60.2 reduce-scatter.26
where the time goes:
time: 1500 us; the launch traced here: 1490 us
  waiting for transfers between devices  993 us (66%)
  blocking collectives  157 us (10%)
  matrix products  144 us (10%)
  other arithmetic  86.3 us (6%)
  local copies, waits for them, and re-layouts  85 us (6%)
  between operations  15.2 us (1%)
    psum x5, waiting for transfers between devices, summed(): return lax.psum(term.astype(jnp.bfloat16), 'narrow').astype(jnp.float32)  459 us
    unnamed x18, waiting for transfers between devices  239 us
    all_to_all x1, blocking collectives, body(): lax.all_to_all(partial_place.astype(jnp.bfloat16), 'wide', split_axis=0,...  96.4 us
    all_to_all x1, waiting for transfers between devices, body(): lax.all_to_all(normed2, 'wide', split_axis=1, concat_axis=0, tiled=True)  93.1 us
    reduce_scatter x1, waiting for transfers between devices, body(): lax.psum_scatter(expand_grad.astype(jnp.bfloat16), 'wide', scatter_dimens...  68.8 us
    reduce_scatter x1, waiting for transfers between devices, body(): lax.psum_scatter(temporal_project_grad.astype(jnp.bfloat16), 'wide', scat...  66.6 us
    reduce_scatter x1, waiting for transfers between devices, body(): lax.psum_scatter(spatial_project_grad.astype(jnp.bfloat16), 'wide', scatt...  66.6 us
    all_to_all x1, blocking collectives, body(): lax.all_to_all(grad_mixed2, 'wide', split_axis=1, concat_axis=0, tiled=True)  31 us
  transfers between devices with their start and end apart: 14, of which 13 were waited for; matrix products, arithmetic and copies ran while one was open for 8% of the time, Pallas kernels for 0%

commit v1 on v0

v1 whole, which is shorter than its diff:
```python
import jax
import jax.numpy as jnp
from jax import lax
from jax.sharding import PartitionSpec as P

HD = 64
FRAMES = 16
GROUP = 16

EPSILON = 1e-06
NEGATIVE = -1e30
HIGHEST = lax.Precision.HIGHEST
SCORE = "fqhd,fkhd->fhqk"
OUT = "fhqk,fkhd->fqhd"
KEY = "fhqk,fqhd->fkhd"
F32 = jnp.float32
BF16 = jnp.bfloat16


def dot(form, *terms):
    return jnp.einsum(form, *terms, preferred_element_type=F32)


def normalize(value, gain):
    return value * lax.rsqrt(jnp.mean(value * value, axis=-1, keepdims=True) + EPSILON) * gain


def norm_back(value, gain, incoming):
    _, pullback = jax.vjp(normalize, value, gain)
    return pullback(incoming)


def split_heads(packed):
    shaped = packed.reshape(packed.shape[:-1] + (packed.shape[-1] // HD, HD))
    return (shaped[..., 0, :, :], shaped[..., 1, :, :], shaped[..., 2, :, :])


def scored(queries, key_rows, allowed):
    scores = dot(SCORE, queries, key_rows) * HD ** (-0.5)
    return scores if allowed is None else jnp.where(allowed, scores, NEGATIVE)


def attend(queries, key_rows, value_rows, allowed):
    scores = scored(queries, key_rows, allowed)
    highest = jnp.max(scores, axis=-1, keepdims=True)
    log_total = jnp.log(jnp.sum(jnp.exp(scores - highest), axis=-1, keepdims=True)) + highest
    shares = jnp.exp(scores - log_total).astype(BF16)
    return dot(OUT, shares, value_rows).astype(BF16), log_total


def attend_back(queries, key_rows, value_rows, log_total, grad_mixed, allowed):
    factor = HD ** (-0.5)
    chances = jnp.exp(scored(queries, key_rows, allowed) - log_total)
    grad_values = dot(KEY, chances.astype(BF16), grad_mixed)
    grad_chances = dot(SCORE, grad_mixed, value_rows)
    grad_scores = (
        chances * (grad_chances - jnp.sum(grad_chances * chances, axis=-1, keepdims=True))
    ).astype(BF16)
    grad_queries = dot(OUT, grad_scores, key_rows) * factor
    grad_keys = dot(KEY, grad_scores, queries) * factor
    return jnp.stack([grad_queries, grad_keys, grad_values], axis=-3).astype(BF16)


def swap(value, axis, bit):
    size = lax.axis_size(axis)
    return lax.ppermute(value, axis, [(i, i ^ bit) for i in range(size)])


def pick(value, place, dim):
    return lax.dynamic_index_in_dim(value, place, dim, keepdims=False)


def added(left, right):
    return (left.astype(F32) + right.astype(F32)).astype(BF16)


def halve(value, dim, axis, bit, place):
    received = swap(pick(value, 1 - place, dim), axis, bit)
    return added(pick(value, place, dim), received)


def scatter_wide(value, dim):
    wide = lax.axis_size("wide")
    me = lax.axis_index("wide")
    block = value.shape[dim] // wide
    left, bit = wide, 1
    while left > 1:
        shape = value.shape[:dim] + (left // 2, 2, block) + value.shape[dim + 1 :]
        value = halve(value.reshape(shape), dim + 1, "wide", bit, (me // bit) % 2)
        left, bit = left // 2, bit * 2
        value = value.reshape(value.shape[:dim] + (left * block,) + value.shape[dim + 2 :])
    return value


def gather_narrow(value):
    other = swap(value, "narrow", 2)
    pair = jnp.stack([value, other])
    near = swap(pair, "narrow", 1)
    return jnp.stack([pair[0], near[0], pair[1], near[1]])


def scatter_narrow(value):
    pair = added(value[:2], swap(value[2:], "narrow", 2))
    return added(pair[0], swap(pair[1], "narrow", 1))


def body(
    tokens,
    frame_counts,
    actions,
    action_table,
    norm_gains,
    spatial_project,
    spatial_merge,
    temporal_project,
    temporal_merge,
    expand_weight,
    reduce_weight,
    grad_out,
):
    frames_dev, tokens_frame, width = tokens.shape
    local = spatial_merge.shape[0]
    wide_me, narrow_me = lax.axis_index("wide"), lax.axis_index("narrow")
    x_me, y_me, c_me = wide_me % 2, narrow_me // 2, narrow_me % 2
    span = tokens_frame // 8
    groups = span // GROUP
    rows = 2 * frames_dev * span

    def keep_of(wide_place):
        frame_ids = wide_place * frames_dev + jnp.arange(frames_dev, dtype=jnp.int32)
        clip_places = jnp.arange(frame_counts.shape[0], dtype=jnp.int32)
        clip_count = jnp.sum(
            jnp.where((frame_ids // FRAMES)[:, None] == clip_places[None, :], frame_counts[None, :], 0),
            axis=1,
        )
        return (frame_ids % FRAMES < clip_count).astype(F32)

    def by_place(near, far):
        both = jnp.concatenate([near, far], axis=0)
        both = both.reshape(2 * frames_dev, groups, GROUP, both.shape[-1])
        return both.transpose(1, 0, 2, 3)

    def by_frame(value):
        value = value.reshape(groups, 2 * frames_dev, GROUP, value.shape[-1]).transpose(1, 0, 2, 3)
        return value.reshape(2, frames_dev, span, value.shape[-1])

    def cut(value, x_place, y_place):
        start = (x_place * 4 + y_place * 2 + c_me) * span
        return lax.dynamic_slice_in_dim(value, start, span, axis=1)

    keep_own = keep_of(wide_me)
    keep_far = keep_of(wide_me + 1 - 2 * x_me)
    keep_place = jnp.broadcast_to(
        jnp.concatenate([keep_own, keep_far])[None, :, None], (groups, 2 * frames_dev, GROUP)
    ).reshape(rows, 1)
    choose = (
        actions[:, None] == jnp.arange(action_table.shape[0], dtype=jnp.int32)[None, :]
    ).astype(BF16)
    extra = dot("fa,ad->fd", choose, action_table)

    far_tokens = swap(cut(tokens, 1 - x_me, y_me), "wide", 1)
    far_extra = swap(extra.astype(BF16), "wide", 1).astype(F32)
    merge1_all = gather_narrow(spatial_merge)
    project_all = gather_narrow(temporal_project)
    merge2_all = gather_narrow(temporal_merge)
    expand_pair = jnp.stack([expand_weight, swap(expand_weight, "narrow", 1)])
    reduce_pair = jnp.stack([reduce_weight, swap(reduce_weight, "narrow", 1)])
    grad_far = swap(
        jnp.stack([cut(grad_out, 1 - x_me, y_me), cut(grad_out, 1 - x_me, 1 - y_me)]), "wide", 1
    )

    start = tokens.astype(F32) + extra[:, None, :]
    normed1 = normalize(start, norm_gains[0]).astype(BF16)
    project1 = dot("fsd,dce->fsce", normed1, spatial_project).astype(BF16)
    heads1 = split_heads(project1)
    mixed1, total1 = attend(heads1[0], heads1[1], heads1[2], None)
    mixed1 = mixed1.reshape(frames_dev, tokens_frame, local)

    shaped = mixed1.reshape(frames_dev, 2, tokens_frame // 2, local)
    moved = jnp.stack([pick(shaped, x_me, 1), swap(pick(shaped, 1 - x_me, 1), "wide", 1)])
    moved = moved.reshape(2, frames_dev, 2, tokens_frame // 4, local)
    moved = jnp.stack([pick(moved, y_me, 2), swap(pick(moved, 1 - y_me, 2), "narrow", 2)])
    moved = moved.reshape(2, 2, frames_dev, 2, span, local)
    moved = jnp.stack([pick(moved, c_me, 3), swap(pick(moved, 1 - c_me, 3), "narrow", 1)], axis=1)
    mixed1_all = moved.reshape(4, 2 * frames_dev, groups, GROUP, local).transpose(0, 2, 1, 3, 4)
    mixed1_all = mixed1_all.reshape(4, rows, local)

    start_place = by_place(
        cut(tokens, x_me, y_me).astype(F32) + extra[:, None, :],
        far_tokens.astype(F32) + far_extra[:, None, :],
    ).reshape(rows, width)
    branch1 = dot("nte,ned->td", mixed1_all, merge1_all)
    hidden1 = start_place + keep_place * branch1
    normed2 = normalize(hidden1, norm_gains[1]).astype(BF16)
    project2 = dot("td,ndce->ntce", normed2, project_all).astype(BF16)
    heads2 = split_heads(project2.reshape(4 * groups, 2 * frames_dev * GROUP, 3, local))
    row_ids = jnp.arange(2 * frames_dev * GROUP, dtype=jnp.int32)
    row_place = row_ids % GROUP
    row_frame = (row_ids // GROUP + x_me * frames_dev) % (2 * frames_dev)
    allowed = (row_place[:, None] == row_place[None, :]) & (row_frame[None, :] <= row_frame[:, None])
    mixed2, total2 = attend(heads2[0], heads2[1], heads2[2], allowed)
    mixed2 = mixed2.reshape(4, rows, local)
    branch2 = dot("nte,ned->td", mixed2, merge2_all)
    hidden2 = hidden1 + keep_place * branch2
    normed3 = normalize(hidden2, norm_gains[2]).astype(BF16)

    grad_result = by_place(cut(grad_out, x_me, y_me), grad_far[0]).reshape(rows, width)
    grad_result_far = by_place(cut(grad_out, x_me, 1 - y_me), grad_far[1]).reshape(rows, width)
    normed3_far = swap(normed3, "narrow", 2)

    def feed(normed, grad):
        grad_branch = (keep_place * grad.astype(F32)).astype(BF16)
        inner = dot("td,cde->cte", normed, expand_pair)
        active, gelu_pull = jax.vjp(jax.nn.gelu, inner)
        active = active.astype(BF16)
        branch = dot("cte,ced->td", active, reduce_pair).astype(BF16)
        grad_active = dot("td,ced->cte", grad_branch, reduce_pair)
        grad_inner = gelu_pull(grad_active)[0].astype(BF16)
        grad_normed = dot("cte,cde->td", grad_inner, expand_pair).astype(BF16)
        return grad_branch, active, branch, grad_inner, grad_normed

    grad_branch3, active, branch3, grad_inner, grad_normed3 = feed(normed3, grad_result)
    far = feed(normed3_far, grad_result_far)
    grad_normed3 = grad_normed3.astype(F32) + swap(far[4], "narrow", 2).astype(F32)
    branch3 = branch3.astype(F32) + swap(far[2], "narrow", 2).astype(F32)
    result = (hidden2 + keep_place * branch3).astype(BF16)
    reduce_grad = dot("cte,td->ced", active, grad_branch3) + dot("cte,td->ced", far[1], far[0])
    expand_grad = dot("td,cte->cde", normed3, grad_inner) + dot("td,cte->cde", normed3_far, far[3])
    reduce_grad = reduce_grad.astype(BF16)
    expand_grad = expand_grad.astype(BF16)
    reduce_grad = added(reduce_grad[0], swap(reduce_grad[1], "narrow", 1))
    expand_grad = added(expand_grad[0], swap(expand_grad[1], "narrow", 1))
    reduce_out = scatter_wide(reduce_grad, 1).astype(F32)
    expand_out = scatter_wide(expand_grad, 0).astype(F32)

    result = by_frame(result)
    result = jnp.stack([result[0], swap(result[1], "wide", 1)])
    result = jnp.stack([result, swap(result, "narrow", 2)])
    result = jnp.stack([result, swap(result, "narrow", 1)])

    def in_order(value):
        value = lax.cond(c_me == 0, lambda v: v, lambda v: v[::-1], value)
        value = lax.cond(y_me == 0, lambda v: v, lambda v: v[:, ::-1], value)
        value = lax.cond(x_me == 0, lambda v: v, lambda v: v[:, :, ::-1], value)
        return value.transpose(3, 2, 1, 0, 4, 5).reshape(frames_dev, tokens_frame, width)

    output = in_order(result)

    back_three, gain_three = norm_back(hidden2, norm_gains[2], grad_normed3)
    grad_hidden2 = grad_result.astype(F32) + back_three
    grad_branch2 = (keep_place * grad_hidden2).astype(BF16)
    merge2_grad = dot("nte,td->ned", mixed2, grad_branch2).astype(BF16)
    grad_mixed2 = dot("td,ned->nte", grad_branch2, merge2_all).astype(BF16)
    grad_mixed2 = grad_mixed2.reshape(heads2[0].shape)
    grad_project2 = attend_back(heads2[0], heads2[1], heads2[2], total2, grad_mixed2, allowed)
    grad_project2 = grad_project2.reshape(4, rows, 3, local)
    project2_grad = dot("td,ntce->ndce", normed2, grad_project2).astype(BF16)
    grad_normed2 = dot("ntce,ndce->td", grad_project2, project_all)
    back_two, gain_two = norm_back(hidden1, norm_gains[1], grad_normed2)
    grad_hidden1 = grad_hidden2 + back_two
    grad_branch1 = (keep_place * grad_hidden1).astype(BF16)
    merge1_grad = dot("nte,td->ned", mixed1_all, grad_branch1).astype(BF16)
    grad_mixed1 = dot("td,ned->nte", grad_branch1, merge1_all).astype(BF16)

    moved = grad_mixed1.reshape(2, 2, groups, 2, frames_dev, GROUP, local)
    moved = moved.transpose(0, 1, 3, 4, 2, 5, 6).reshape(2, 2, 2, frames_dev, span, local)
    near, other = moved[:, 0], swap(moved[:, 1], "narrow", 1)
    moved = jnp.stack(
        [jnp.where(c_me == 0, near, other), jnp.where(c_me == 0, other, near)], axis=3
    )
    near, other = moved[0], swap(moved[1], "narrow", 2)
    moved = jnp.stack(
        [jnp.where(y_me == 0, near, other), jnp.where(y_me == 0, other, near)], axis=2
    )
    near, other = moved[0], swap(moved[1], "wide", 1)
    moved = jnp.stack(
        [jnp.where(x_me == 0, near, other), jnp.where(x_me == 0, other, near)], axis=1
    )
    grad_mixed1 = moved.reshape(heads1[0].shape)

    hidden_parts = by_frame(grad_hidden1.astype(BF16))
    grad_hidden_own = jnp.stack([hidden_parts[0], swap(hidden_parts[1], "wide", 1)], axis=1)

    grad_project1 = attend_back(heads1[0], heads1[1], heads1[2], total1, grad_mixed1, None)
    grad_project1 = grad_project1.reshape(frames_dev, tokens_frame, 3, local)
    project1_grad = dot("fsd,fsce->dce", normed1, grad_project1).astype(BF16)
    partial = dot("fsce,dce->fsd", grad_project1, spatial_project).astype(BF16)
    partial = partial.reshape(frames_dev, 2, 2, 2, span, width)
    partial = halve(partial, 3, "narrow", 1, c_me)
    partial = halve(partial, 2, "narrow", 2, y_me)
    grad_normed1 = jnp.stack([pick(partial, x_me, 1), pick(partial, 1 - x_me, 1)], axis=1).astype(F32)
    start_own = (
        jnp.stack([cut(tokens, x_me, y_me), cut(tokens, 1 - x_me, y_me)], axis=1).astype(F32)
        + extra[:, None, None, :]
    )
    back_one, gain_one = norm_back(start_own, norm_gains[0], grad_normed1)
    grad_start = grad_hidden_own.astype(F32) + back_one
    frame_totals = jnp.sum(grad_start, axis=(1, 2))
    table_grad = jnp.dot(choose.astype(F32).T, frame_totals, precision=HIGHEST)
    grad_part = grad_start.astype(BF16).transpose(1, 0, 2, 3)
    grad_part = jnp.stack([grad_part, swap(grad_part, "narrow", 2)])
    grad_part = jnp.stack([grad_part, swap(grad_part, "narrow", 1)])
    grad_tokens = in_order(grad_part).astype(F32)

    small = jnp.concatenate([jnp.stack([gain_one, gain_two, gain_three]), table_grad])
    small = small + swap(small, "narrow", 1)
    small = small + swap(small, "narrow", 2)
    wide = lax.axis_size("wide")
    bit = 1
    while bit < wide:
        small = small + swap(small, "wide", bit)
        bit *= 2
    small = lax.dynamic_slice_in_dim(small, wide_me * (width // wide), width // wide, axis=1)

    project2_out = scatter_wide(scatter_narrow(project2_grad), 0).astype(F32)
    merge2_out = scatter_wide(scatter_narrow(merge2_grad), 1).astype(F32)
    merge1_out = scatter_wide(scatter_narrow(merge1_grad), 1).astype(F32)
    project1_out = scatter_wide(project1_grad, 0).astype(F32)
    return (
        output,
        grad_tokens,
        small[:3],
        small[3:],
        project1_out,
        merge1_out,
        project2_out,
        merge2_out,
        expand_out,
        reduce_out,
    )


def solution(mesh):
    return jax.shard_map(
        body,
        mesh=mesh,
        in_specs=(
            P("wide", None, None),
            P(),
            P("wide"),
            P(),
            P(),
            P(None, None, "narrow"),
            P("narrow", None),
            P(None, None, "narrow"),
            P("narrow", None),
            P(None, "narrow"),
            P("narrow", None),
            P("wide", None, None),
        ),
        out_specs=(
            P("wide", None, None),
            P("wide", None, None),
            P(None, "wide"),
            P(None, "wide"),
            P("wide", None, "narrow"),
            P("narrow", "wide"),
            P("wide", None, "narrow"),
            P("narrow", "wide"),
            P("wide", "narrow"),
            P("narrow", "wide"),
        ),
        check_vma=False,
    )
```

time: 1500 us -> 786 us (0.52)
  the two profiles are of different devices: /device:TPU:0 before, /device:TPU:31 now
where the time goes in v1:
time: 786 us; the launch traced here: 774 us
  waiting for transfers between devices  249 us (32%)
  local copies, waits for them, and re-layouts  209 us (27%)
  matrix products  160 us (20%)
  other arithmetic  89.9 us (11%)
  starting transfers between devices  63.5 us (8%)
    ppermute x59, waiting for transfers between devices, swap(): return lax.ppermute(value, axis, [(i, i ^ bit) for i in range(size)])  249 us
    dot_general x37, matrix products, dot(): return jnp.einsum(form, *terms, preferred_element_type=F32)  159 us
    ppermute x59, starting transfers between devices, swap(): return lax.ppermute(value, axis, [(i, i ^ bit) for i in range(size)])  63.5 us
    unnamed x227, local copies, waits for them, and re-layouts  35.6 us
    cond x6, local copies, waits for them, and re-layouts  30.1 us
    another operation x10, local copies, waits for them, and re-layouts, attend_back(): jnp.stack([grad_queries, grad_keys, grad_values], axis=-3).astype(BF16)  28.4 us
    convert_element_type x22, other arithmetic, added(): return (left.astype(F32) + right.astype(F32)).astype(BF16)  24.6 us
    dynamic_slice x11, local copies, waits for them, and re-layouts, pick(): return lax.dynamic_index_in_dim(value, place, dim, keepdims=False)  17.5 us
  transfers between devices with their start and end apart: 59, of which 17 were waited for; matrix products, arithmetic and copies ran while one was open for 51% of the time, Pallas kernels for 0%

profile of v1, /device:TPU:31, one launch (start us, length us, event | category | flops | bytes accessed | tf_op | source)
XLA Modules:
  0.0 774.3 jit_solution(5164058566022398063)
XLA Ops:
  17.0 4.1 convolution_convert_fusion
  38.2 4.1 copy.180
  69.6 8.2 %collective-permute-done.3 = bf16[2,8,64,256]{3,2,1,0:T(8,128)(2,1)S(1)} collective-permute-done((bf16[2,8,64,256]{3,2,1,0:T(8,128)(2,1)S(1)}, bf16[2,8,64,256]{3,2,1,0:T(8,128)(2,1)S(1)}, u32[]{:S(2)}, u32[]{:S(2)}) %collective-permute-start.3) | collective-permute-done | bytes 524320 | tf_op jit(solution)/shard_map/ppermute | solution.py:66
  87.1 5.1 convert_bitcast_fusion.2
  92.2 4.1 copy.173
  96.3 5.9 reshape_reshape.31
  121.6 4.7 fusion.79
  126.4 5.9 fusion.71
  132.3 6.6 fusion.11
  139.0 5.7 fusion.77
  144.7 4.7 bitcast_convert_fusion.5
  149.4 4.6 fusion.75
  154.1 6.2 bitcast_convert_fusion.4
  160.6 6.8 fusion.18
  167.5 4.6 bitcast_convert_fusion.2
  173.4 7.4 add_convert_fusion
  184.8 5.8 fusion.20
  192.3 14.5 %collective-permute-done.19 = bf16[512,1024]{1,0:T(8,128)(2,1)S(1)} collective-permute-done((bf16[512,1024]{1,0:T(8,128)(2,1)S(1)}, bf16[512,1024]{1,0:T(8,128)(2,1)S(1)}, u32[]{:S(2)}, u32[]{:S(2)}) %collective-permute-start.19) | collective-permute-done | bytes 1048608 | tf_op jit(solution)/shard_map/ppermute | solution.py:66
  206.8 5.7 multiply_reduce_fusion.4
  223.3 6.9 fusion.58
  230.2 5.5 multiply_reduce_fusion.1
  242.8 4.1 copy.284
  246.9 4.3 reshape.513
  253.7 4.4 reshape.511
  260.6 4.6 reshape.512
  268.5 6.1 fusion.44
  274.6 5.5 convert_bitcast_fusion.1
  309.4 19.3 %collective-permute-done.36 = bf16[2,256,1024]{2,1,0:T(8,128)(2,1)S(1)} collective-permute-done((bf16[2,256,1024]{2,1,0:T(8,128)(2,1)S(1)}, bf16[2,256,1024]{2,1,0:T(8,128)(2,1)S(1)}, u32[]{:S(2)}, u32[]{:S(2)}) %collective-permute-start.36) | collective-permute-done | bytes 1048608 | tf_op jit(solution)/shard_map/ppermute | solution.py:66
  330.5 5.6 collective-permute-start.47
  348.1 81.9 %collective-permute-done.22 = bf16[2,8,2,32,256]{4,3,1,0,2:T(8,128)(2,1)} collective-permute-done((bf16[2,8,2,32,256]{4,3,1,0,2:T(8,128)(2,1)S(1)}, bf16[2,8,2,32,256]{4,3,1,0,2:T(8,128)(2,1)}, u32[]{:S(2)}, u32[]{:S(2)}) %collective-permute-start.22) | collective-permute-done | bytes 524320 | tf_op jit(solution)/shard_map/ppermute | solution.py:66
  447.5 38.2 %collective-permute-done.23 = bf16[8,2,2,32,256]{4,3,0,2,1:T(8,128)(2,1)} collective-permute-done((bf16[8,2,2,32,256]{4,3,0,2,1:T(8,128)(2,1)}, bf16[8,2,2,32,256]{4,3,0,2,1:T(8,128)(2,1)}, u32[]{:S(2)}, u32[]{:S(2)}) %collective-permute-start.23) | collective-permute-done | bytes 524320 | tf_op jit(solution)/shard_map/ppermute | solution.py:66
  492.1 6.1 convolution_convert_fusion.3
  498.2 4.8 multiply_reduce_fusion
  515.6 6.7 bitcast_convert_fusion.1
  527.5 7.5 collective-permute-start.24
  544.5 4.5 collective-permute-done.50
  559.1 19.2 %collective-permute-done.33 = bf16[4,128,3,256]{3,1,2,0:T(8,128)(2,1)S(1)} collective-permute-done((bf16[4,128,3,256]{3,1,2,0:T(8,128)(2,1)S(1)}, bf16[4,128,3,256]{3,1,2,0:T(8,128)(2,1)S(1)}, u32[]{:S(2)}, u32[]{:S(2)}) %collective-permute-start.33) | collective-permute-done | bytes 786464 | tf_op jit(solution)/shard_map/ppermute | solution.py:66
  578.3 6.5 collective-permute-start.17
  588.0 10.7 %collective-permute-done.53 = bf16[2,128,1024]{2,1,0:T(8,128)(2,1)S(1)} collective-permute-done((bf16[2,128,1024]{2,1,0:T(8,128)(2,1)S(1)}, bf16[2,128,1024]{2,1,0:T(8,128)(2,1)S(1)}, u32[]{:S(2)}, u32[]{:S(2)}) %collective-permute-start.53) | collective-permute-done | bytes 524320 | tf_op jit(solution)/shard_map/ppermute | solution.py:66
  604.3 17.9 %collective-permute-done.25 = bf16[8,2,32,1024]{3,2,0,1:T(8,128)(2,1)S(1)} collective-permute-done((bf16[8,2,32,1024]{3,2,0,1:T(8,128)(2,1)S(1)}, bf16[8,2,32,1024]{3,2,0,1:T(8,128)(2,1)S(1)}, u32[]{:S(2)}, u32[]{:S(2)}) %collective-permute-start.25) | collective-permute-done | bytes 1048608 | tf_op jit(solution)/shard_map/ppermute | solution.py:66
  637.2 4.9 constant_dynamic-slice_fusion.9
  642.1 4.6 copy.311
  649.1 7.3 collective-permute-done.26
  679.5 9.0 %collective-permute-done.31 = f32[11,1024]{1,0:T(8,128)S(1)} collective-permute-done((f32[11,1024]{1,0:T(8,128)S(1)}, f32[11,1024]{1,0:T(8,128)S(1)}, u32[]{:S(2)}, u32[]{:S(2)}) %collective-permute-start.31) | collective-permute-done | bytes 45088 | tf_op jit(solution)/shard_map/ppermute | solution.py:66
  695.1 10.0 %conditional.6 = (bf16[2,2,2,8,32,1024]{5,4,3,2,1,0:T(8,128)(2,1)}) conditional(s32[]{:T(128)} %convert_element_type.571, bf16[2,2,2,8,32,1024]{5,4,3,2,1,0:T(8,128)(2,1)} %pad_maximum_fusion.3, bf16[2,2,2,8,32,1024]{5,4,3,2,1,0:T(8,128)(2,1)} %pad_maximum_fusion.3), branch_computations={%region_9.10_spmd, %region_10.11_spmd} | conditional | bytes 16777224 | solution.py:242
  695.1 5.0 copy.389
  700.1 5.0 rev.12
  705.1 10.0 %conditional.7 = (bf16[2,2,2,8,32,1024]{5,4,3,2,1,0:T(8,128)(2,1)}) conditional(s32[]{:T(128)} %convert_element_type.570, bf16[2,2,2,8,32,1024]{5,4,3,2,1,0:T(8,128)(2,1)} %get-tuple-element.136, bf16[2,2,2,8,32,1024]{5,4,3,2,1,0:T(8,128)(2,1)} %get-tuple-element.136), branch_computations={%region_11.12_spmd, %region_12.13_spmd} | conditional | bytes 16777224 | solution.py:243
  705.1 5.0 copy.390
  710.1 5.0 rev.13
  715.2 10.0 %conditional.8 = (bf16[2,2,2,8,32,1024]{5,4,3,2,1,0:T(8,128)(2,1)}) conditional(s32[]{:T(128)} %convert_element_type.569, bf16[2,2,2,8,32,1024]{5,4,3,2,1,0:T(8,128)(2,1)} %get-tuple-element.137, bf16[2,2,2,8,32,1024]{5,4,3,2,1,0:T(8,128)(2,1)} %get-tuple-element.137), branch_computations={%region_13.14_spmd, %region_14.15_spmd} | conditional | bytes 16777224 | solution.py:244
  715.2 5.0 copy.391
  720.2 5.0 rev.14
  725.2 5.2 copy.186
  736.3 10.0 %conditional.9 = (bf16[2,2,2,8,32,1024]{5,4,3,2,1,0:T(8,128)(2,1)}) conditional(s32[]{:T(128)} %convert_element_type.571, bf16[2,2,2,8,32,1024]{5,4,3,2,1,0:T(8,128)(2,1)} %pad_maximum_fusion.4, bf16[2,2,2,8,32,1024]{5,4,3,2,1,0:T(8,128)(2,1)} %pad_maximum_fusion.4), branch_computations={%region_21.22_spmd, %region_22.23_spmd} | conditional | bytes 16777224 | solution.py:242
  736.3 5.0 copy.392
  741.3 5.0 rev.15
  746.3 10.0 %conditional.10 = (bf16[2,2,2,8,32,1024]{5,4,3,2,1,0:T(8,128)(2,1)}) conditional(s32[]{:T(128)} %convert_element_type.570, bf16[2,2,2,8,32,1024]{5,4,3,2,1,0:T(8,128)(2,1)} %get-tuple-element.139, bf16[2,2,2,8,32,1024]{5,4,3,2,1,0:T(8,128)(2,1)} %get-tuple-element.139), branch_computations={%region_23.24_spmd, %region_24.25_spmd} | conditional | bytes 16777224 | solution.py:243
  746.3 5.0 copy.393
  751.3 5.0 rev.16
  756.4 10.0 %conditional.11 = (bf16[2,2,2,8,32,1024]{5,4,3,2,1,0:T(8,128)(2,1)}) conditional(s32[]{:T(128)} %convert_element_type.569, bf16[2,2,2,8,32,1024]{5,4,3,2,1,0:T(8,128)(2,1)} %get-tuple-element.140, bf16[2,2,2,8,32,1024]{5,4,3,2,1,0:T(8,128)(2,1)} %get-tuple-element.140), branch_computations={%region_25.26_spmd, %region_26.27_spmd} | conditional | bytes 16777224 | solution.py:244
  756.4 5.0 copy.394
  761.4 5.0 rev.17
  769.6 4.2 copy.224
  (513 shorter events, 290.4 us)
Async XLA Ops:
  1.7 34.0 %copy-start.60 = (f32[8,1024]{1,0:T(8,128)}, f32[8,1024]{1,0:T(8,128)S(1)}, u32[]{:S(2)}) copy-start(f32[8,1024]{1,0:T(8,128)S(1)} %get-tuple-element.115) | copy-start | bytes 98308
  1.7 47.8 %collective-permute-start.1 = (bf16[8,1024]{1,0:T(8,128)(2,1)S(1)}, bf16[8,1024]{1,0:T(8,128)(2,1)S(1)}, u32[]{:S(2)}, u32[]{:S(2)}) collective-permute-start(bf16[8,1024]{1,0:T(8,128)(2,1)S(1)} %get-tuple-element.114), channel_id=1, source_target_pairs={{0,4},{4,0},{8,12},{12,8},{16,20},{20,16},{24,28},{28,24},{1,5},{5... | collective-permute-start | bytes 49160 | tf_op jit(solution)/shard_map/ppermute | solution.py:66
  2.0 62.8 %collective-permute-start.5 = (bf16[256,1024]{1,0:T(8,128)(2,1)}, bf16[256,1024]{1,0:T(8,128)(2,1)}, u32[]{:S(2)}, u32[]{:S(2)}) collective-permute-start(bf16[256,1024]{1,0:T(8,128)(2,1)} %param.30), channel_id=1, source_target_pairs={{0,2},{1,3},{2,0},{3,1},{4,6},{5,7},{6,4},{7,5},{8,10},{9,11},{10,... | collective-permute-start | bytes 1572872 | tf_op jit(solution)/shard_map/ppermute | solution.py:66
  4.3 29.2 %copy-start.13 = (bf16[8,1,32,1024]{3,2,0,1:T(8,128)(2,1)}, bf16[8,1,32,1024]{3,2,0,1:T(8,128)(2,1)S(1)}, u32[]{:S(2)}) copy-start(bf16[8,1,32,1024]{3,2,0,1:T(8,128)(2,1)S(1)} %get-tuple-element.58) | copy-start | bytes 1572868
  4.3 48.5 %collective-permute-start = (bf16[8,32,1024]{2,1,0:T(8,128)(2,1)}, bf16[8,32,1024]{2,1,0:T(8,128)(2,1)}, u32[]{:S(2)}, u32[]{:S(2)}) collective-permute-start(bf16[8,32,1024]{2,1,0:T(8,128)(2,1)} %get-tuple-element.59), channel_id=1, source_target_pairs={{0,4},{4,0},{8,12},{12,8},{16,20},{20,16},{24,28},{28,24},{1,5},{5... | collective-permute-start | bytes 1572872 | tf_op jit(solution)/shard_map/ppermute | solution.py:66
  8.1 41.7 %collective-permute-start.7 = (bf16[1024,3,256]{0,2,1:T(8,128)(2,1)}, bf16[1024,3,256]{0,2,1:T(8,128)(2,1)}, u32[]{:S(2)}, u32[]{:S(2)}) collective-permute-start(bf16[1024,3,256]{0,2,1:T(8,128)(2,1)} %copy.171), channel_id=1, source_target_pairs={{0,2},{1,3},{2,0},{3,1},{4,6},{5,7},{6,4},{7,5},{8,10},{9,11},{10,... | collective-permute-start | bytes 4718600 | tf_op jit(solution)/shard_map/ppermute | solution.py:66
  13.1 54.1 %collective-permute-start.18 = (bf16[2,8,32,1024]{3,2,1,0:T(8,128)(2,1)}, bf16[2,8,32,1024]{3,2,1,0:T(8,128)(2,1)}, u32[]{:S(2)}, u32[]{:S(2)}) collective-permute-start(bf16[2,8,32,1024]{3,2,1,0:T(8,128)(2,1)} %pad_maximum_fusion.18), channel_id=1, source_target_pairs={{0,4},{4,0},{8,12},{12,8},{16,20},{20,16},{24,28},{28,24},{1,5},{5... | collective-permute-start | bytes 3145736 | tf_op jit(solution)/shard_map/ppermute | solution.py:66
  49.5 15.0 %collective-permute-start.9 = (bf16[256,1024]{1,0:T(8,128)(2,1)}, bf16[256,1024]{1,0:T(8,128)(2,1)S(1)}, u32[]{:S(2)}, u32[]{:S(2)}) collective-permute-start(bf16[256,1024]{1,0:T(8,128)(2,1)} %param.32), channel_id=1, source_target_pairs={{0,2},{1,3},{2,0},{3,1},{4,6},{5,7},{6,4},{7,5},{8,10},{9,11},{10,... | collective-permute-start | bytes 1572872 | tf_op jit(solution)/shard_map/ppermute | solution.py:66
  49.8 11.3 %collective-permute-start.2 = (bf16[8,128,256]{2,1,0:T(8,128)(2,1)}, bf16[8,128,256]{2,1,0:T(8,128)(2,1)S(1)}, u32[]{:S(2)}, u32[]{:S(2)}) collective-permute-start(bf16[8,128,256]{2,1,0:T(8,128)(2,1)} %bitcast.612), channel_id=1, source_target_pairs={{0,4},{4,0},{8,12},{12,8},{16,20},{20,16},{24,28},{28,24},{1,5},{5... | collective-permute-start | bytes 1572872 | tf_op jit(solution)/shard_map/ppermute | solution.py:66
  52.8 32.8 %collective-permute-start.8 = (bf16[2,1024,3,256]{1,3,2,0:T(8,128)(2,1)S(1)}, bf16[2,1024,3,256]{1,3,2,0:T(8,128)(2,1)S(1)}, u32[]{:S(2)}, u32[]{:S(2)}) collective-permute-start(bf16[2,1024,3,256]{1,3,2,0:T(8,128)(2,1)S(1)} %pad_maximum_fusion.5), channel_id=1, source_target_pairs={{0,1},{1,0},{2,3},{3,2},{4,5},{5,4},{6,7},{7,6},{8,9},{9,8},{10,11... | collective-permute-start | bytes 9437192 | tf_op jit(solution)/shard_map/ppermute | solution.py:66
  61.1 60.6 %collective-permute-start.11 = (bf16[1024,1024]{0,1:T(8,128)(2,1)}, bf16[1024,1024]{0,1:T(8,128)(2,1)}, u32[]{:S(2)}, u32[]{:S(2)}) collective-permute-start(bf16[1024,1024]{0,1:T(8,128)(2,1)} %copy.180), channel_id=1, source_target_pairs={{0,1},{1,0},{2,3},{3,2},{4,5},{5,4},{6,7},{7,6},{8,9},{9,8},{10,11... | collective-permute-start | bytes 6291464 | tf_op jit(solution)/shard_map/ppermute | solution.py:66
  64.5 67.8 %collective-permute-start.12 = (bf16[1024,1024]{1,0:T(8,128)(2,1)}, bf16[1024,1024]{1,0:T(8,128)(2,1)}, u32[]{:S(2)}, u32[]{:S(2)}) collective-permute-start(bf16[1024,1024]{1,0:T(8,128)(2,1)} %param.34), channel_id=1, source_target_pairs={{0,1},{1,0},{2,3},{3,2},{4,5},{5,4},{6,7},{7,6},{8,9},{9,8},{10,11... | collective-permute-start | bytes 6291464 | tf_op jit(solution)/shard_map/ppermute | solution.py:66
  64.7 13.1 %collective-permute-start.3 = (bf16[2,8,64,256]{3,2,1,0:T(8,128)(2,1)S(1)}, bf16[2,8,64,256]{3,2,1,0:T(8,128)(2,1)S(1)}, u32[]{:S(2)}, u32[]{:S(2)}) collective-permute-start(bf16[2,8,64,256]{3,2,1,0:T(8,128)(2,1)S(1)} %get-tuple-element.101), channel_id=1, source_target_pairs={{0,2},{1,3},{2,0},{3,1},{4,6},{5,7},{6,4},{7,5},{8,10},{9,11},{10,... | collective-permute-start | bytes 1572872 | tf_op jit(solution)/shard_map/ppermute | solution.py:66
  67.2 14.3 %collective-permute-start.6 = (bf16[2,256,1024]{2,1,0:T(8,128)(2,1)S(1)}, bf16[2,256,1024]{2,1,0:T(8,128)(2,1)S(1)}, u32[]{:S(2)}, u32[]{:S(2)}) collective-permute-start(bf16[2,256,1024]{2,1,0:T(8,128)(2,1)S(1)} %pad_maximum_fusion.15), channel_id=1, source_target_pairs={{0,1},{1,0},{2,3},{3,2},{4,5},{5,4},{6,7},{7,6},{8,9},{9,8},{10,11... | collective-permute-start | bytes 3145736 | tf_op jit(solution)/shard_map/ppermute | solution.py:66
  77.9 3.3 collective-permute-start.4
  81.2 3.3 collective-permute-start.10
  120.3 29.1 %collective-permute-start.13 = (bf16[512,1024]{1,0:T(8,128)(2,1)S(1)}, bf16[512,1024]{1,0:T(8,128)(2,1)S(1)}, u32[]{:S(2)}, u32[]{:S(2)}) collective-permute-start(bf16[512,1024]{1,0:T(8,128)(2,1)S(1)} %multiply_convert_fusion.9), channel_id=1, source_target_pairs={{0,2},{1,3},{2,0},{3,1},{4,6},{5,7},{6,4},{7,5},{8,10},{9,11},{10,... | collective-permute-start | bytes 3145736 | tf_op jit(solution)/shard_map/ppermute | solution.py:66
  160.3 52.1 %collective-permute-start.14 = (bf16[512,1024]{1,0:T(8,128)(2,1)S(1)}, bf16[512,1024]{1,0:T(8,128)(2,1)S(1)}, u32[]{:S(2)}, u32[]{:S(2)}) collective-permute-start(bf16[512,1024]{1,0:T(8,128)(2,1)S(1)} %bitcast_convert_fusion.4), channel_id=1, source_target_pairs={{0,2},{1,3},{2,0},{3,1},{4,6},{5,7},{6,4},{7,5},{8,10},{9,11},{10,... | collective-permute-start | bytes 3145736 | tf_op jit(solution)/shard_map/ppermute | solution.py:66
  172.1 34.7 %collective-permute-start.19 = (bf16[512,1024]{1,0:T(8,128)(2,1)S(1)}, bf16[512,1024]{1,0:T(8,128)(2,1)S(1)}, u32[]{:S(2)}, u32[]{:S(2)}) collective-permute-start(bf16[512,1024]{1,0:T(8,128)(2,1)S(1)} %bitcast_convert_fusion.2), channel_id=1, source_target_pairs={{0,2},{1,3},{2,0},{3,1},{4,6},{5,7},{6,4},{7,5},{8,10},{9,11},{10,... | collective-permute-start | bytes 3145736 | tf_op jit(solution)/shard_map/ppermute | solution.py:66
  183.4 146.8 %collective-permute-start.55 = (bf16[1024,1024]{0,1:T(8,128)(2,1)}, bf16[1024,1024]{0,1:T(8,128)(2,1)}, u32[]{:S(2)}, u32[]{:S(2)}) collective-permute-start(bf16[1024,1024]{0,1:T(8,128)(2,1)} %slice_bitcast_fusion), channel_id=1, source_target_pairs={{0,1},{1,0},{2,3},{3,2},{4,5},{5,4},{6,7},{7,6},{8,9},{9,8},{10,11... | collective-permute-start | bytes 6291464 | tf_op jit(solution)/shard_map/ppermute | solution.py:66
  192.3 152.6 %collective-permute-start.51 = (bf16[1024,1024]{1,0:T(8,128)(2,1)}, bf16[1024,1024]{1,0:T(8,128)(2,1)}, u32[]{:S(2)}, u32[]{:S(2)}) collective-permute-start(bf16[1024,1024]{1,0:T(8,128)(2,1)} %slice_bitcast_fusion.2), channel_id=1, source_target_pairs={{0,1},{1,0},{2,3},{3,2},{4,5},{5,4},{6,7},{7,6},{8,9},{9,8},{10,11... | collective-permute-start | bytes 6291464 | tf_op jit(solution)/shard_map/ppermute | solution.py:66
  281.1 21.8 %collective-permute-start.15 = (bf16[8,32,1024]{2,1,0:T(8,128)(2,1)}, bf16[8,32,1024]{2,1,0:T(8,128)(2,1)}, u32[]{:S(2)}, u32[]{:S(2)}) collective-permute-start(bf16[8,32,1024]{2,1,0:T(8,128)(2,1)} %bitcast.55), channel_id=1, source_target_pairs={{0,4},{4,0},{8,12},{12,8},{16,20},{20,16},{24,28},{28,24},{1,5},{5... | collective-permute-start | bytes 1572872 | tf_op jit(solution)/shard_map/ppermute | solution.py:66
  283.3 23.0 %collective-permute-start.46 = (bf16[2,256,1024]{2,1,0:T(8,128)(2,1)}, bf16[2,256,1024]{2,1,0:T(8,128)(2,1)}, u32[]{:S(2)}, u32[]{:S(2)}) collective-permute-start(bf16[2,256,1024]{2,1,0:T(8,128)(2,1)} %slice.225), channel_id=1, source_target_pairs={{0,2},{1,3},{2,0},{3,1},{4,6},{5,7},{6,4},{7,5},{8,10},{9,11},{10,... | collective-permute-start | bytes 3145736 | tf_op jit(solution)/shard_map/ppermute | solution.py:66
  292.0 9.5 %collective-permute-start.21 = (bf16[2,2,8,32,256]{4,3,2,1,0:T(8,128)(2,1)S(1)}, bf16[2,2,8,32,256]{4,3,2,1,0:T(8,128)(2,1)S(1)}, u32[]{:S(2)}, u32[]{:S(2)}) collective-permute-start(bf16[2,2,8,32,256]{4,3,2,1,0:T(8,128)(2,1)S(1)} %slice_bitcast_fusion.19), channel_id=1, source_target_pairs={{0,1},{1,0},{2,3},{3,2},{4,5},{5,4},{6,7},{7,6},{8,9},{9,8},{10,11... | collective-permute-start | bytes 1572872 | tf_op jit(solution)/shard_map/ppermute | solution.py:66
  301.5 27.2 %collective-permute-start.36 = (bf16[2,256,1024]{2,1,0:T(8,128)(2,1)S(1)}, bf16[2,256,1024]{2,1,0:T(8,128)(2,1)S(1)}, u32[]{:S(2)}, u32[]{:S(2)}) collective-permute-start(bf16[2,256,1024]{2,1,0:T(8,128)(2,1)S(1)} %slice.217), channel_id=1, source_target_pairs={{0,2},{1,3},{2,0},{3,1},{4,6},{5,7},{6,4},{7,5},{8,10},{9,11},{10,... | collective-permute-start | bytes 3145736 | tf_op jit(solution)/shard_map/ppermute | solution.py:66
  302.9 297.8 %collective-permute-start.41 = (bf16[2,1024,3,256]{1,3,2,0:T(8,128)(2,1)}, bf16[2,1024,3,256]{1,3,2,0:T(8,128)(2,1)}, u32[]{:S(2)}, u32[]{:S(2)}) collective-permute-start(bf16[2,1024,3,256]{1,3,2,0:T(8,128)(2,1)} %slice.221), channel_id=1, source_target_pairs={{0,2},{1,3},{2,0},{3,1},{4,6},{5,7},{6,4},{7,5},{8,10},{9,11},{10,... | collective-permute-start | bytes 9437192 | tf_op jit(solution)/shard_map/ppermute | solution.py:66
  306.4 136.5 %collective-permute-start.16 = (bf16[2,8,32,1024]{3,2,1,0:T(8,128)(2,1)}, bf16[2,8,32,1024]{3,2,1,0:T(8,128)(2,1)}, u32[]{:S(2)}, u32[]{:S(2)}) collective-permute-start(bf16[2,8,32,1024]{3,2,1,0:T(8,128)(2,1)} %get-tuple-element.92), channel_id=1, source_target_pairs={{0,2},{1,3},{2,0},{3,1},{4,6},{5,7},{6,4},{7,5},{8,10},{9,11},{10,... | collective-permute-start | bytes 3145736 | tf_op jit(solution)/shard_map/ppermute | solution.py:66
  328.7 101.2 %collective-permute-start.22 = (bf16[2,8,2,32,256]{4,3,1,0,2:T(8,128)(2,1)S(1)}, bf16[2,8,2,32,256]{4,3,1,0,2:T(8,128)(2,1)}, u32[]{:S(2)}, u32[]{:S(2)}) collective-permute-start(bf16[2,8,2,32,256]{4,3,1,0,2:T(8,128)(2,1)S(1)} %fusion.105), channel_id=1, source_target_pairs={{0,2},{1,3},{2,0},{3,1},{4,6},{5,7},{6,4},{7,5},{8,10},{9,11},{10,... | collective-permute-start | bytes 1572872 | tf_op jit(solution)/shard_map/ppermute | solution.py:66
  330.5 102.9 %collective-permute-start.47 = (bf16[256,1024]{1,0:T(8,128)(2,1)}, bf16[256,1024]{1,0:T(8,128)(2,1)}, u32[]{:S(2)}, u32[]{:S(2)}) collective-permute-start(bf16[256,1024]{1,0:T(8,128)(2,1)} %slice_bitcast_fusion.15), channel_id=1, source_target_pairs={{0,1},{1,0},{2,3},{3,2},{4,5},{5,4},{6,7},{7,6},{8,9},{9,8},{10,11... | collective-permute-start | bytes 1572872 | tf_op jit(solution)/shard_map/ppermute | solution.py:66
  344.9 93.3 %collective-permute-start.37 = (bf16[256,1024]{1,0:T(8,128)(2,1)}, bf16[256,1024]{1,0:T(8,128)(2,1)}, u32[]{:S(2)}, u32[]{:S(2)}) collective-permute-start(bf16[256,1024]{1,0:T(8,128)(2,1)} %slice_bitcast_fusion.17), channel_id=1, source_target_pairs={{0,1},{1,0},{2,3},{3,2},{4,5},{5,4},{6,7},{7,6},{8,9},{9,8},{10,11... | collective-permute-start | bytes 1572872 | tf_op jit(solution)/shard_map/ppermute | solution.py:66
  348.1 85.3 %copy-start.9 = (bf16[1024,1024]{1,0:T(8,128)(2,1)}, bf16[1024,1024]{1,0:T(8,128)(2,1)S(1)}, u32[]{:S(2)}) copy-start(bf16[1024,1024]{1,0:T(8,128)(2,1)S(1)} %fusion.22) | copy-start | bytes 6291460
  429.9 125.5 %collective-permute-start.56 = (bf16[1024,4,128]{2,0,1:T(8,128)(2,1)}, bf16[1024,4,128]{2,0,1:T(8,128)(2,1)}, u32[]{:S(2)}, u32[]{:S(2)}) collective-permute-start(bf16[1024,4,128]{2,0,1:T(8,128)(2,1)} %bitcast.190), channel_id=1, source_target_pairs={{0,4},{4,0},{8,12},{12,8},{16,20},{20,16},{24,28},{28,24},{1,5},{5... | collective-permute-start | bytes 3145736 | tf_op jit(solution)/shard_map/ppermute | solution.py:66
  433.4 123.9 %collective-permute-start.52 = (bf16[4,128,1024]{2,1,0:T(8,128)(2,1)}, bf16[4,128,1024]{2,1,0:T(8,128)(2,1)}, u32[]{:S(2)}, u32[]{:S(2)}) collective-permute-start(bf16[4,128,1024]{2,1,0:T(8,128)(2,1)} %dynamic-slice_bitcast_fusion), channel_id=1, source_target_pairs={{0,4},{4,0},{8,12},{12,8},{16,20},{20,16},{24,28},{28,24},{1,5},{5... | collective-permute-start | bytes 3145736 | tf_op jit(solution)/shard_map/ppermute | solution.py:66
  438.2 47.6 %collective-permute-start.23 = (bf16[8,2,2,32,256]{4,3,0,2,1:T(8,128)(2,1)}, bf16[8,2,2,32,256]{4,3,0,2,1:T(8,128)(2,1)}, u32[]{:S(2)}, u32[]{:S(2)}) collective-permute-start(bf16[8,2,2,32,256]{4,3,0,2,1:T(8,128)(2,1)} %fusion.104), channel_id=1, source_target_pairs={{0,4},{4,0},{8,12},{12,8},{16,20},{20,16},{24,28},{28,24},{1,5},{5... | collective-permute-start | bytes 1572872 | tf_op jit(solution)/shard_map/ppermute | solution.py:66
  442.8 84.7 %collective-permute-start.48 = (bf16[256,4,128]{2,0,1:T(8,128)(2,1)S(1)}, bf16[256,4,128]{2,0,1:T(8,128)(2,1)}, u32[]{:S(2)}, u32[]{:S(2)}) collective-permute-start(bf16[256,4,128]{2,0,1:T(8,128)(2,1)S(1)} %bitcast.632), channel_id=1, source_target_pairs={{0,4},{4,0},{8,12},{12,8},{16,20},{20,16},{24,28},{28,24},{1,5},{5... | collective-permute-start | bytes 786440 | tf_op jit(solution)/shard_map/ppermute | solution.py:66
  444.0 42.0 %copy-start.23 = (bf16[2,8,1,2,32,256]{5,4,1,0,3,2:T(8,128)(2,1)S(1)}, bf16[2,8,1,2,32,256]{5,4,1,0,3,2:T(8,128)(2,1)}, u32[]{:S(2)}) copy-start(bf16[2,8,1,2,32,256]{5,4,1,0,3,2:T(8,128)(2,1)} %copy-done.22) | copy-start | bytes 1572868
  485.8 50.4 %collective-permute-start.38 = (bf16[256,4,128]{2,0,1:T(8,128)(2,1)}, bf16[256,4,128]{2,0,1:T(8,128)(2,1)}, u32[]{:S(2)}, u32[]{:S(2)}) collective-permute-start(bf16[256,4,128]{2,0,1:T(8,128)(2,1)} %bitcast.543), channel_id=1, source_target_pairs={{0,4},{4,0},{8,12},{12,8},{16,20},{20,16},{24,28},{28,24},{1,5},{5... | collective-permute-start | bytes 786440 | tf_op jit(solution)/shard_map/ppermute | solution.py:66
  527.5 57.8 %collective-permute-start.24 = (bf16[8,2,2,32,1024]{4,3,0,1,2:T(8,128)(2,1)S(1)}, bf16[8,2,2,32,1024]{4,3,0,1,2:T(8,128)(2,1)S(1)}, u32[]{:S(2)}, u32[]{:S(2)}) collective-permute-start(bf16[8,2,2,32,1024]{4,3,0,1,2:T(8,128)(2,1)S(1)} %bitcast.591), channel_id=1, source_target_pairs={{0,1},{1,0},{2,3},{3,2},{4,5},{5,4},{6,7},{7,6},{8,9},{9,8},{10,11... | collective-permute-start | bytes 6291464 | tf_op jit(solution)/shard_map/ppermute | solution.py:66
  536.1 4.4 collective-permute-start.49
  540.6 3.8 collective-permute-start.39
  544.4 4.6 collective-permute-start.50
  549.0 4.6 collective-permute-start.40
  553.6 73.4 %collective-permute-start.20 = (bf16[8,32,1024]{2,1,0:T(8,128)(2,1)S(1)}, bf16[8,32,1024]{2,1,0:T(8,128)(2,1)S(1)}, u32[]{:S(2)}, u32[]{:S(2)}) collective-permute-start(bf16[8,32,1024]{2,1,0:T(8,128)(2,1)S(1)} %bitcast.613), channel_id=1, source_target_pairs={{0,4},{4,0},{8,12},{12,8},{16,20},{20,16},{24,28},{28,24},{1,5},{5... | collective-permute-start | bytes 1572872 | tf_op jit(solution)/shard_map/ppermute | solution.py:66
  555.5 22.8 %collective-permute-start.33 = (bf16[4,128,3,256]{3,1,2,0:T(8,128)(2,1)S(1)}, bf16[4,128,3,256]{3,1,2,0:T(8,128)(2,1)S(1)}, u32[]{:S(2)}, u32[]{:S(2)}) collective-permute-start(bf16[4,128,3,256]{3,1,2,0:T(8,128)(2,1)S(1)} %bitcast.610), channel_id=1, source_target_pairs={{0,4},{4,0},{8,12},{12,8},{16,20},{20,16},{24,28},{28,24},{1,5},{5... | collective-permute-start | bytes 2359304 | tf_op jit(solution)/shard_map/ppermute | solution.py:66
  557.3 27.8 %collective-permute-start.57 = (bf16[1024,2,128]{2,0,1:T(8,128)(2,1)S(1)}, bf16[1024,2,128]{2,0,1:T(8,128)(2,1)S(1)}, u32[]{:S(2)}, u32[]{:S(2)}) collective-permute-start(bf16[1024,2,128]{2,0,1:T(8,128)(2,1)S(1)} %dynamic-slice_bitcast_fusion.2), channel_id=1, source_target_pairs={{0,8},{4,12},{8,0},{12,4},{16,24},{20,28},{24,16},{28,20},{1,9},{5... | collective-permute-start | bytes 1572872 | tf_op jit(solution)/shard_map/ppermute | solution.py:66
  559.0 41.7 %slice-start.6 = ((s8[6291456]{0:T(1024)(128)(4,1)}), s8[4194304]{0:T(1024)(128)(4,1)S(1)}, s32[]{:S(2)}) async-start(s8[6291456]{0:T(1024)(128)(4,1)} %bitcast.566), calls=%async_computation.6 | async-start | bytes 8388608
  578.3 112.8 %collective-permute-start.17 = (bf16[2,2,8,32,1024]{4,3,2,1,0:T(8,128)(2,1)}, bf16[2,2,8,32,1024]{4,3,2,1,0:T(8,128)(2,1)}, u32[]{:S(2)}, u32[]{:S(2)}) collective-permute-start(bf16[2,2,8,32,1024]{4,3,2,1,0:T(8,128)(2,1)} %get-tuple-element.74), channel_id=1, source_target_pairs={{0,1},{1,0},{2,3},{3,2},{4,5},{5,4},{6,7},{7,6},{8,9},{9,8},{10,11... | collective-permute-start | bytes 6291464 | tf_op jit(solution)/shard_map/ppermute | solution.py:66
  585.1 13.6 %collective-permute-start.53 = (bf16[2,128,1024]{2,1,0:T(8,128)(2,1)S(1)}, bf16[2,128,1024]{2,1,0:T(8,128)(2,1)S(1)}, u32[]{:S(2)}, u32[]{:S(2)}) collective-permute-start(bf16[2,128,1024]{2,1,0:T(8,128)(2,1)S(1)} %dynamic-slice_bitcast_fusion.3), channel_id=1, source_target_pairs={{0,8},{4,12},{8,0},{12,4},{16,24},{20,28},{24,16},{28,20},{1,9},{5... | collective-permute-start | bytes 1572872 | tf_op jit(solution)/shard_map/ppermute | solution.py:66
  585.3 45.9 %collective-permute-start.34 = (bf16[2,128,3,256]{3,1,2,0:T(8,128)(2,1)S(1)}, bf16[2,128,3,256]{3,1,2,0:T(8,128)(2,1)S(1)}, u32[]{:S(2)}, u32[]{:S(2)}) collective-permute-start(bf16[2,128,3,256]{3,1,2,0:T(8,128)(2,1)S(1)} %dynamic-slice_bitcast_fusion.8), channel_id=1, source_target_pairs={{0,8},{4,12},{8,0},{12,4},{16,24},{20,28},{24,16},{28,20},{1,9},{5... | collective-permute-start | bytes 1179656 | tf_op jit(solution)/shard_map/ppermute | solution.py:66
  598.7 23.5 %collective-permute-start.25 = (bf16[8,2,32,1024]{3,2,0,1:T(8,128)(2,1)S(1)}, bf16[8,2,32,1024]{3,2,0,1:T(8,128)(2,1)S(1)}, u32[]{:S(2)}, u32[]{:S(2)}) collective-permute-start(bf16[8,2,32,1024]{3,2,0,1:T(8,128)(2,1)S(1)} %dynamic-slice_bitcast_fusion.1), channel_id=1, source_target_pairs={{0,2},{1,3},{2,0},{3,1},{4,6},{5,7},{6,4},{7,5},{8,10},{9,11},{10,... | collective-permute-start | bytes 3145736 | tf_op jit(solution)/shard_map/ppermute | solution.py:66
  600.7 61.0 %collective-permute-start.58 = (bf16[1024,1,128]{2,0,1:T(8,128)(2,1)}, bf16[1024,1,128]{2,0,1:T(8,128)(2,1)}, u32[]{:S(2)}, u32[]{:S(2)}) collective-permute-start(bf16[1024,1,128]{2,0,1:T(8,128)(2,1)} %constant_dynamic-slice_fusion), channel_id=1, source_target_pairs={{0,16},{4,20},{8,24},{12,28},{16,0},{20,4},{24,8},{28,12},{1,17},{... | collective-permute-start | bytes 786440 | tf_op jit(solution)/shard_map/ppermute | solution.py:66
  622.2 10.1 %collective-permute-start.42 = (bf16[1024,3,256]{0,2,1:T(8,128)(2,1)S(1)}, bf16[1024,3,256]{0,2,1:T(8,128)(2,1)S(1)}, u32[]{:S(2)}, u32[]{:S(2)}) collective-permute-start(bf16[1024,3,256]{0,2,1:T(8,128)(2,1)S(1)} %slice_bitcast_fusion.4), channel_id=1, source_target_pairs={{0,1},{1,0},{2,3},{3,2},{4,5},{5,4},{6,7},{7,6},{8,9},{9,8},{10,11... | collective-permute-start | bytes 4718600 | tf_op jit(solution)/shard_map/ppermute | solution.py:66
  627.0 45.8 %collective-permute-start.54 = (bf16[1,128,1024]{2,1,0:T(8,128)(2,1)}, bf16[1,128,1024]{2,1,0:T(8,128)(2,1)}, u32[]{:S(2)}, u32[]{:S(2)}) collective-permute-start(bf16[1,128,1024]{2,1,0:T(8,128)(2,1)} %constant_dynamic-slice_fusion.3), channel_id=1, source_target_pairs={{0,16},{4,20},{8,24},{12,28},{16,0},{20,4},{24,8},{28,12},{1,17},{... | collective-permute-start | bytes 786440 | tf_op jit(solution)/shard_map/ppermute | solution.py:66
  631.2 25.1 %collective-permute-start.26 = (bf16[2,8,32,1024]{3,2,1,0:T(8,128)(2,1)}, bf16[2,8,32,1024]{3,2,1,0:T(8,128)(2,1)}, u32[]{:S(2)}, u32[]{:S(2)}) collective-permute-start(bf16[2,8,32,1024]{3,2,1,0:T(8,128)(2,1)} %get-tuple-element.70), channel_id=1, source_target_pairs={{0,2},{1,3},{2,0},{3,1},{4,6},{5,7},{6,4},{7,5},{8,10},{9,11},{10,... | collective-permute-start | bytes 3145736 | tf_op jit(solution)/shard_map/ppermute | solution.py:66
  646.8 23.0 %collective-permute-start.43 = (bf16[4,128,3,256]{3,1,2,0:T(8,128)(2,1)}, bf16[4,128,3,256]{3,1,2,0:T(8,128)(2,1)}, u32[]{:S(2)}, u32[]{:S(2)}) collective-permute-start(bf16[4,128,3,256]{3,1,2,0:T(8,128)(2,1)} %bitcast.159), channel_id=1, source_target_pairs={{0,4},{4,0},{8,12},{12,8},{16,20},{20,16},{24,28},{28,24},{1,5},{5... | collective-permute-start | bytes 2359304 | tf_op jit(solution)/shard_map/ppermute | solution.py:66
  656.3 4.7 collective-permute-start.28
  661.0 71.3 %collective-permute-start.27 = (bf16[2,2,8,32,1024]{4,3,2,1,0:T(8,128)(2,1)}, bf16[2,2,8,32,1024]{4,3,2,1,0:T(8,128)(2,1)}, u32[]{:S(2)}, u32[]{:S(2)}) collective-permute-start(bf16[2,2,8,32,1024]{4,3,2,1,0:T(8,128)(2,1)} %get-tuple-element.68), channel_id=1, source_target_pairs={{0,1},{1,0},{2,3},{3,2},{4,5},{5,4},{6,7},{7,6},{8,9},{9,8},{10,11... | collective-permute-start | bytes 6291464 | tf_op jit(solution)/shard_map/ppermute | solution.py:66
  661.7 4.9 collective-permute-start.29
  666.6 12.1 %collective-permute-start.35 = (bf16[1,128,3,256]{3,1,2,0:T(8,128)(2,1)}, bf16[1,128,3,256]{3,1,2,0:T(8,128)(2,1)S(1)}, u32[]{:S(2)}, u32[]{:S(2)}) collective-permute-start(bf16[1,128,3,256]{3,1,2,0:T(8,128)(2,1)} %constant_dynamic-slice_fusion.13), channel_id=1, source_target_pairs={{0,16},{4,20},{8,24},{12,28},{16,0},{20,4},{24,8},{28,12},{1,17},{... | collective-permute-start | bytes 589832 | tf_op jit(solution)/shard_map/ppermute | solution.py:66
  669.8 5.0 collective-permute-start.30
  672.7 15.8 %collective-permute-start.44 = (bf16[2,128,3,256]{3,1,2,0:T(8,128)(2,1)S(1)}, bf16[2,128,3,256]{3,1,2,0:T(8,128)(2,1)S(1)}, u32[]{:S(2)}, u32[]{:S(2)}) collective-permute-start(bf16[2,128,3,256]{3,1,2,0:T(8,128)(2,1)S(1)} %dynamic-slice_bitcast_fusion.7), channel_id=1, source_target_pairs={{0,8},{4,12},{8,0},{12,4},{16,24},{20,28},{24,16},{28,20},{1,9},{5... | collective-permute-start | bytes 1179656 | tf_op jit(solution)/shard_map/ppermute | solution.py:66
  674.8 13.6 %collective-permute-start.31 = (f32[11,1024]{1,0:T(8,128)S(1)}, f32[11,1024]{1,0:T(8,128)S(1)}, u32[]{:S(2)}, u32[]{:S(2)}) collective-permute-start(f32[11,1024]{1,0:T(8,128)S(1)} %add.569), channel_id=1, source_target_pairs={{0,8},{4,12},{8,0},{12,4},{16,24},{20,28},{24,16},{28,20},{1,9},{5... | collective-permute-start | bytes 135176 | tf_op jit(solution)/shard_map/ppermute | solution.py:66
  688.5 41.9 %collective-permute-start.32 = (f32[11,1024]{1,0:T(8,128)S(1)}, f32[11,1024]{1,0:T(8,128)S(1)}, u32[]{:S(2)}, u32[]{:S(2)}) collective-permute-start(f32[11,1024]{1,0:T(8,128)S(1)} %add.570), channel_id=1, source_target_pairs={{0,16},{4,20},{8,24},{12,28},{16,0},{20,4},{24,8},{28,12},{1,17},{... | collective-permute-start | bytes 135176 | tf_op jit(solution)/shard_map/ppermute | solution.py:66
  688.7 42.8 %collective-permute-start.45 = (bf16[1,128,3,256]{3,1,2,0:T(8,128)(2,1)S(1)}, bf16[1,128,3,256]{3,1,2,0:T(8,128)(2,1)S(1)}, u32[]{:S(2)}, u32[]{:S(2)}) collective-permute-start(bf16[1,128,3,256]{3,1,2,0:T(8,128)(2,1)S(1)} %constant_dynamic-slice_fusion.7), channel_id=1, source_target_pairs={{0,16},{4,20},{8,24},{12,28},{16,0},{20,4},{24,8},{28,12},{1,17},{... | collective-permute-start | bytes 589832 | tf_op jit(solution)/shard_map/ppermute | solution.py:66
  (103 other events, 764.2 us)

commit v2 on v1

v2 whole, which is shorter than its diff:
```python
import jax
import jax.numpy as jnp
from jax import lax
from jax.experimental import pallas as pl
from jax.experimental.pallas import tpu as pltpu
from jax.sharding import PartitionSpec as P

HD = 64
FRAMES = 16
GROUP = 16
PAIR = 2 * HD

EPSILON = 1e-06
NEGATIVE = -1e30
HIGHEST = lax.Precision.HIGHEST
F32 = jnp.float32
BF16 = jnp.bfloat16
VMEM_LIMIT = 56 * 1024 * 1024
NN = (((1,), (0,)), ((), ()))
NT = (((1,), (1,)), ((), ()))
TN = (((0,), (0,)), ((), ()))


def mm(left, right, form=NN):
    return lax.dot_general(left, right, form, preferred_element_type=F32)


def root(value):
    return lax.rsqrt(jnp.mean(value * value, axis=-1, keepdims=True) + EPSILON)


def norm_back(value, gain, incoming):
    scale = root(value)
    scaled = gain * incoming
    inner = jnp.mean(scaled * value, axis=-1, keepdims=True)
    back = scale * scaled - (scale * scale * scale) * inner * value
    return back, jnp.sum(incoming * value * scale, axis=0, keepdims=True)


def sides():
    lane = lax.broadcasted_iota(jnp.int32, (1, PAIR), 1)
    low = (lane < HD).astype(F32)
    return lane < HD, low.astype(BF16), (1.0 - low).astype(BF16)


def attend_pair(queries, key_rows, value_rows, allowed):
    is_low, low, high = sides()
    mixed = []
    for side in (low, high):
        scores = mm(queries * (side * HD ** (-0.5)), key_rows, NT)
        if allowed is not None:
            scores = jnp.where(allowed, scores, NEGATIVE)
        shares = jnp.exp(scores - jnp.max(scores, axis=-1, keepdims=True))
        shares = shares * (1.0 / jnp.sum(shares, axis=-1, keepdims=True))
        mixed.append(mm(shares.astype(BF16), value_rows))
    return jnp.where(is_low, mixed[0], mixed[1]).astype(BF16)


def attend_back_pair(queries, key_rows, value_rows, grad_mixed, allowed):
    factor = HD ** (-0.5)
    is_low, low, high = sides()
    parts = []
    for side in (low, high):
        scores = mm(key_rows, queries * (side * factor), NT)
        if allowed is not None:
            scores = jnp.where(allowed, scores, NEGATIVE)
        chances = jnp.exp(scores - jnp.max(scores, axis=0, keepdims=True))
        chances = chances * (1.0 / jnp.sum(chances, axis=0, keepdims=True))
        grad_chances = mm(value_rows, grad_mixed * side, NT)
        shift = jnp.sum(grad_chances * chances, axis=0, keepdims=True)
        grad_scores = (chances * (grad_chances - shift)).astype(BF16)
        parts.append(
            (
                mm(grad_scores, key_rows, TN) * factor,
                mm(grad_scores, queries) * factor,
                mm(chances.astype(BF16), grad_mixed),
            )
        )
    return [jnp.where(is_low, a, b).astype(BF16) for a, b in zip(parts[0], parts[1])]


def whole(shape):
    return pl.BlockSpec(shape, lambda *_: (0,) * len(shape))


def call(kernel, grid, in_specs, out_specs, out_shape, scratch=(), flops=0, moved=0):
    return pl.pallas_call(
        kernel,
        grid=grid,
        in_specs=in_specs,
        out_specs=out_specs,
        out_shape=out_shape,
        scratch_shapes=list(scratch),
        compiler_params=pltpu.CompilerParams(vmem_limit_bytes=VMEM_LIMIT),
        cost_estimate=pl.CostEstimate(flops=flops, bytes_accessed=moved, transcendentals=0),
    )


def shape_of(shape, kind=BF16):
    return jax.ShapeDtypeStruct(shape, kind)


def spatial_forward(tokens, extra, gain, project):
    frames, places, width = tokens.shape
    local = project.shape[-1]

    def kernel(tokens_ref, extra_ref, gain_ref, project_ref, normed_ref, heads_ref, mixed_ref):
        start = tokens_ref[0].astype(F32) + extra_ref[0]
        normed = (start * root(start) * gain_ref[...]).astype(BF16)
        normed_ref[0] = normed
        for c in range(3):
            heads_ref[c, 0] = mm(normed, project_ref[c]).astype(BF16)
        for at in range(0, local, PAIR):
            part = pl.ds(at, PAIR)
            mixed_ref[0, :, part] = attend_pair(
                heads_ref[0, 0, :, part], heads_ref[1, 0, :, part], heads_ref[2, 0, :, part], None
            )

    return call(
        kernel,
        (frames,),
        [
            pl.BlockSpec((1, places, width), lambda f: (f, 0, 0)),
            pl.BlockSpec((1, 1, width), lambda f: (f, 0, 0)),
            whole((1, width)),
            whole(project.shape),
        ],
        [
            pl.BlockSpec((1, places, width), lambda f: (f, 0, 0)),
            pl.BlockSpec((3, 1, places, local), lambda f: (0, f, 0, 0)),
            pl.BlockSpec((1, places, local), lambda f: (f, 0, 0)),
        ],
        [
            shape_of((frames, places, width)),
            shape_of((3, frames, places, local)),
            shape_of((frames, places, local)),
        ],
        flops=2 * frames * places * width * local * 4,
        moved=12 * 2**20,
    )(tokens, extra[:, None, :], gain, project)


def place_masks(x_me, frames_all, transposed):
    rows = frames_all * GROUP
    shape = (rows, rows)
    query = lax.broadcasted_iota(jnp.int32, shape, 1 if transposed else 0)
    key = lax.broadcasted_iota(jnp.int32, shape, 0 if transposed else 1)
    query_frame = (query // GROUP + x_me * (frames_all // 2)) % frames_all
    key_frame = (key // GROUP + x_me * (frames_all // 2)) % frames_all
    return (query % GROUP == key % GROUP) & (key_frame <= query_frame)


def temporal_forward(begin, keep, gains, mixed1, merge1, project, merge2):
    rows, width = begin.shape
    local = mixed1.shape[-1]
    group_rows = FRAMES * GROUP

    def kernel(
        begin_ref,
        keep_ref,
        gains_ref,
        mixed1_ref,
        merge1_ref,
        project_ref,
        merge2_ref,
        hidden1_ref,
        normed2_ref,
        heads_ref,
        mixed2_ref,
        hidden2_ref,
        normed3_ref,
    ):
        step = pl.program_id(0)
        keep_rows = keep_ref[...]

        @pl.when(step == 0)
        def _():
            branch = mm(mixed1_ref[0], merge1_ref[0])
            for n in range(1, 4):
                branch += mm(mixed1_ref[n], merge1_ref[n])
            hidden1 = begin_ref[...] + keep_rows * branch
            hidden1_ref[...] = hidden1
            hidden2_ref[...] = hidden1
            normed2_ref[...] = (hidden1 * root(hidden1) * gains_ref[1:2]).astype(BF16)

        for c in range(3):
            heads_ref[0, c] = mm(normed2_ref[...], project_ref[0, c]).astype(BF16)
        allowed = place_masks(lax.axis_index("wide") % 2, FRAMES, False)
        for g in range(rows // group_rows):
            band = pl.ds(g * group_rows, group_rows)
            for at in range(0, local, PAIR):
                part = pl.ds(at, PAIR)
                mixed2_ref[0, band, part] = attend_pair(
                    heads_ref[0, 0, band, part],
                    heads_ref[0, 1, band, part],
                    heads_ref[0, 2, band, part],
                    allowed,
                )
        hidden2_ref[...] += keep_rows * mm(mixed2_ref[0], merge2_ref[0])

        @pl.when(step == 3)
        def _():
            hidden2 = hidden2_ref[...]
            normed3_ref[...] = (hidden2 * root(hidden2) * gains_ref[2:3]).astype(BF16)

    return call(
        kernel,
        (4,),
        [
            whole((rows, width)),
            whole((rows, 1)),
            whole((3, width)),
            whole((4, rows, local)),
            whole((4, local, width)),
            pl.BlockSpec((1, 3, width, local), lambda n: (n, 0, 0, 0)),
            pl.BlockSpec((1, local, width), lambda n: (n, 0, 0)),
        ],
        [
            whole((rows, width)),
            whole((rows, width)),
            pl.BlockSpec((1, 3, rows, local), lambda n: (n, 0, 0, 0)),
            pl.BlockSpec((1, rows, local), lambda n: (n, 0, 0)),
            whole((rows, width)),
            whole((rows, width)),
        ],
        [
            shape_of((rows, width), F32),
            shape_of((rows, width)),
            shape_of((4, 3, rows, local)),
            shape_of((4, rows, local)),
            shape_of((rows, width), F32),
            shape_of((rows, width)),
        ],
        flops=2 * rows * width * width * 6,
        moved=24 * 2**20,
    )(begin, keep, gains, mixed1, merge1, project, merge2)


RATE = 0.7978845608028654
CUBIC = 0.044715


def feed_forward(normed, grad, keep, expand, reduce):
    rows, width = normed.shape
    cores, _, units = expand.shape
    block = 512
    per = units // block

    def kernel(
        normed_ref,
        grad_ref,
        keep_ref,
        expand_ref,
        reduce_ref,
        active_ref,
        inner_ref,
        grad_branch_ref,
        branch_ref,
        grad_normed_ref,
        branch_sum,
        grad_sum,
    ):
        step = pl.program_id(0)

        @pl.when(step == 0)
        def _():
            grad_branch_ref[...] = (keep_ref[...] * grad_ref[...].astype(F32)).astype(BF16)
            branch_sum[...] = jnp.zeros_like(branch_sum)
            grad_sum[...] = jnp.zeros_like(grad_sum)

        inner = mm(normed_ref[...], expand_ref[0])
        grad_active = mm(grad_branch_ref[...], reduce_ref[0], NT)
        square = inner * inner
        bend = jnp.tanh(RATE * inner * (1.0 + CUBIC * square))
        half = 0.5 * (1.0 + bend)
        active = (inner * half).astype(BF16)
        slope = half + (0.5 * RATE) * inner * (1.0 - bend * bend) * (1.0 + (3.0 * CUBIC) * square)
        grad_inner = (grad_active * slope).astype(BF16)
        active_ref[...] = active
        inner_ref[...] = grad_inner
        branch_sum[...] += mm(active, reduce_ref[0])
        grad_sum[...] += mm(grad_inner, expand_ref[0], NT)

        @pl.when(step == cores * per - 1)
        def _():
            branch_ref[...] = branch_sum[...].astype(BF16)
            grad_normed_ref[...] = grad_sum[...].astype(BF16)

    full = whole((rows, width))
    return call(
        kernel,
        (cores * per,),
        [
            full,
            full,
            whole((rows, 1)),
            pl.BlockSpec((1, width, block), lambda j: (j // per, 0, j % per)),
            pl.BlockSpec((1, block, width), lambda j: (j // per, j % per, 0)),
        ],
        [
            pl.BlockSpec((rows, block), lambda j: (0, j)),
            pl.BlockSpec((rows, block), lambda j: (0, j)),
            full,
            full,
            full,
        ],
        [
            shape_of((rows, cores * units)),
            shape_of((rows, cores * units)),
            shape_of((rows, width)),
            shape_of((rows, width)),
            shape_of((rows, width)),
        ],
        scratch=[pltpu.VMEM((rows, width), F32), pltpu.VMEM((rows, width), F32)],
        flops=8 * rows * width * cores * units,
        moved=18 * 2**20,
    )(normed, grad, keep, expand, reduce)


def outer(pairs, blocks, left_map, right_map, out_map, left_block, right_block, out_shape, flops):
    count = len(pairs)

    def kernel(*refs):
        total = mm(refs[0][...].reshape(refs[0].shape[-2:]), refs[1][...].reshape(refs[1].shape[-2:]), TN)
        for i in range(1, count):
            left, right = refs[2 * i], refs[2 * i + 1]
            total += mm(left[...].reshape(left.shape[-2:]), right[...].reshape(right.shape[-2:]), TN)
        out = refs[-1]
        out[...] = total.astype(BF16).reshape(out.shape)

    specs = []
    for left, right in pairs:
        specs += [pl.BlockSpec(left_block, left_map), pl.BlockSpec(right_block, right_map)]
    out_block = (1,) * (len(out_shape) - 2) + (left_block[-1], right_block[-1])
    return call(
        kernel,
        blocks,
        specs,
        pl.BlockSpec(out_block, out_map),
        shape_of(out_shape),
        flops=flops,
        moved=16 * 2**20,
    )(*[term for pair in pairs for term in pair])


def temporal_backward(
    grad_near, grad_far, hidden2, hidden1, grad_result, keep, gains, heads, merge2, project, merge1
):
    rows, width = hidden1.shape
    local = merge1.shape[1]
    group_rows = FRAMES * GROUP

    def kernel(
        near_ref,
        far_ref,
        hidden2_ref,
        hidden1_ref,
        result_ref,
        keep_ref,
        gains_ref,
        heads_ref,
        merge2_ref,
        project_ref,
        merge1_ref,
        branch2_ref,
        grad_heads_ref,
        branch1_ref,
        mixed1_ref,
        carried_ref,
        gain3_ref,
        gain2_ref,
        grad_hidden,
        grad_normed,
        grad_mixed,
    ):
        step = pl.program_id(0)

        @pl.when(step == 0)
        def _():
            incoming = near_ref[...].astype(F32) + far_ref[...].astype(F32)
            back, gain3_ref[...] = norm_back(hidden2_ref[...], gains_ref[2:3], incoming)
            total = result_ref[...].astype(F32) + back
            grad_hidden[...] = total
            branch2_ref[...] = (keep_ref[...] * total).astype(BF16)
            grad_normed[...] = jnp.zeros_like(grad_normed)

        grad_mixed[...] = mm(branch2_ref[...], merge2_ref[0], NT).astype(BF16)
        allowed = place_masks(lax.axis_index("wide") % 2, FRAMES, True)
        for g in range(rows // group_rows):
            band = pl.ds(g * group_rows, group_rows)
            for at in range(0, local, PAIR):
                part = pl.ds(at, PAIR)
                grads = attend_back_pair(
                    heads_ref[0, 0, band, part],
                    heads_ref[0, 1, band, part],
                    heads_ref[0, 2, band, part],
                    grad_mixed[band, part],
                    allowed,
                )
                for c in range(3):
                    grad_heads_ref[0, c, band, part] = grads[c]
        total = mm(grad_heads_ref[0, 0], project_ref[0, 0], NT)
        for c in range(1, 3):
            total += mm(grad_heads_ref[0, c], project_ref[0, c], NT)
        grad_normed[...] += total

        @pl.when(step == 3)
        def _():
            back, gain2_ref[...] = norm_back(hidden1_ref[...], gains_ref[1:2], grad_normed[...])
            total = grad_hidden[...] + back
            carried_ref[...] = total.astype(BF16)
            branch1_ref[...] = (keep_ref[...] * total).astype(BF16)
            for n in range(4):
                mixed1_ref[n] = mm(branch1_ref[...], merge1_ref[n], NT).astype(BF16)

    full = whole((rows, width))
    row = whole((1, width))
    return call(
        kernel,
        (4,),
        [
            full,
            full,
            full,
            full,
            full,
            whole((rows, 1)),
            whole((3, width)),
            pl.BlockSpec((1, 3, rows, local), lambda n: (n, 0, 0, 0)),
            pl.BlockSpec((1, local, width), lambda n: (n, 0, 0)),
            pl.BlockSpec((1, 3, width, local), lambda n: (n, 0, 0, 0)),
            whole((4, local, width)),
        ],
        [
            full,
            pl.BlockSpec((1, 3, rows, local), lambda n: (n, 0, 0, 0)),
            full,
            whole((4, rows, local)),
            full,
            row,
            row,
        ],
        [
            shape_of((rows, width)),
            shape_of((4, 3, rows, local)),
            shape_of((rows, width)),
            shape_of((4, rows, local)),
            shape_of((rows, width)),
            shape_of((1, width), F32),
            shape_of((1, width), F32),
        ],
        scratch=[
            pltpu.VMEM((rows, width), F32),
            pltpu.VMEM((rows, width), F32),
            pltpu.VMEM((rows, local), BF16),
        ],
        flops=2 * rows * width * width * 8,
        moved=30 * 2**20,
    )(grad_near, grad_far, hidden2, hidden1, grad_result, keep, gains, heads, merge2, project, merge1)


def spatial_backward(heads, grad_mixed, project):
    _, frames, places, local = heads.shape
    width = project.shape[1]

    def kernel(heads_ref, mixed_ref, project_ref, grad_heads_ref, partial_ref):
        for at in range(0, local, PAIR):
            part = pl.ds(at, PAIR)
            grads = attend_back_pair(
                heads_ref[0, 0, :, part],
                heads_ref[1, 0, :, part],
                heads_ref[2, 0, :, part],
                mixed_ref[0, :, part],
                None,
            )
            for c in range(3):
                grad_heads_ref[c, 0, :, part] = grads[c]
        total = mm(grad_heads_ref[0, 0], project_ref[0], NT)
        for c in range(1, 3):
            total += mm(grad_heads_ref[c, 0], project_ref[c], NT)
        partial_ref[0] = total.astype(BF16)

    return call(
        kernel,
        (frames,),
        [
            pl.BlockSpec((3, 1, places, local), lambda f: (0, f, 0, 0)),
            pl.BlockSpec((1, places, local), lambda f: (f, 0, 0)),
            whole(project.shape),
        ],
        [
            pl.BlockSpec((3, 1, places, local), lambda f: (0, f, 0, 0)),
            pl.BlockSpec((1, places, width), lambda f: (f, 0, 0)),
        ],
        [shape_of((3, frames, places, local)), shape_of((frames, places, width))],
        flops=2 * frames * places * width * local * 5,
        moved=14 * 2**20,
    )(heads, grad_mixed, project)


def in_order(value, kind):
    _, _, _, frames, span, width = value.shape
    wide_me, narrow_me = lax.axis_index("wide"), lax.axis_index("narrow")
    me = jnp.stack([narrow_me % 2, narrow_me // 2, wide_me % 2]).astype(jnp.int32)

    def kernel(me_ref, value_ref, out_ref):
        out_ref[...] = value_ref[0, 0, 0].astype(kind)

    return pl.pallas_call(
        kernel,
        grid_spec=pltpu.PrefetchScalarGridSpec(
            num_scalar_prefetch=1,
            grid=(2, 2, 2),
            in_specs=[
                pl.BlockSpec((1, 1, 1, frames, span, width), lambda c, y, x, me: (c, y, x, 0, 0, 0))
            ],
            out_specs=pl.BlockSpec(
                (frames, span, width),
                lambda c, y, x, me: (0, (x ^ me[2]) * 4 + (y ^ me[1]) * 2 + (c ^ me[0]), 0),
            ),
        ),
        out_shape=shape_of((frames, 8 * span, width), kind),
        compiler_params=pltpu.CompilerParams(vmem_limit_bytes=VMEM_LIMIT),
        cost_estimate=pl.CostEstimate(flops=0, bytes_accessed=12 * 2**20, transcendentals=0),
    )(me, value)


def swap(value, axis, bit):
    size = lax.axis_size(axis)
    return lax.ppermute(value, axis, [(i, i ^ bit) for i in range(size)])


def pick(value, place, dim):
    return lax.dynamic_index_in_dim(value, place, dim, keepdims=False)


def added(left, right):
    return (left.astype(F32) + right.astype(F32)).astype(BF16)


def after(value, *earlier):
    return lax.optimization_barrier((value,) + earlier)[0]


def halve(value, dim, axis, bit, place):
    received = swap(pick(value, 1 - place, dim), axis, bit)
    return added(pick(value, place, dim), received)


def scatter_wide(value, dim):
    wide = lax.axis_size("wide")
    me = lax.axis_index("wide")
    block = value.shape[dim] // wide
    left, bit = wide, 1
    while left > 1:
        shape = value.shape[:dim] + (left // 2, 2, block) + value.shape[dim + 1 :]
        value = halve(value.reshape(shape), dim + 1, "wide", bit, (me // bit) % 2)
        left, bit = left // 2, bit * 2
        value = value.reshape(value.shape[:dim] + (left * block,) + value.shape[dim + 2 :])
    return value


def gather_narrow(value):
    other = swap(value, "narrow", 2)
    pair = jnp.stack([value, other])
    near = swap(pair, "narrow", 1)
    return jnp.stack([pair[0], near[0], pair[1], near[1]])


def scatter_narrow(value):
    pair = added(value[:2], swap(value[2:], "narrow", 2))
    return added(pair[0], swap(pair[1], "narrow", 1))


def body(
    tokens,
    frame_counts,
    actions,
    action_table,
    norm_gains,
    spatial_project,
    spatial_merge,
    temporal_project,
    temporal_merge,
    expand_weight,
    reduce_weight,
    grad_out,
):
    frames_dev, tokens_frame, width = tokens.shape
    local = spatial_merge.shape[0]
    wide_me, narrow_me = lax.axis_index("wide"), lax.axis_index("narrow")
    x_me, y_me, c_me = wide_me % 2, narrow_me // 2, narrow_me % 2
    span = tokens_frame // 8
    groups = span // GROUP
    rows = 2 * frames_dev * span
    spatial_project = spatial_project.transpose(1, 0, 2)
    temporal_project = temporal_project.transpose(1, 0, 2)

    def keep_of(wide_place):
        frame_ids = wide_place * frames_dev + jnp.arange(frames_dev, dtype=jnp.int32)
        clip_places = jnp.arange(frame_counts.shape[0], dtype=jnp.int32)
        clip_count = jnp.sum(
            jnp.where((frame_ids // FRAMES)[:, None] == clip_places[None, :], frame_counts[None, :], 0),
            axis=1,
        )
        return (frame_ids % FRAMES < clip_count).astype(F32)

    def by_place(near, far):
        both = jnp.concatenate([near, far], axis=0)
        both = both.reshape(2 * frames_dev, groups, GROUP, both.shape[-1])
        return both.transpose(1, 0, 2, 3).reshape(rows, both.shape[-1])

    def by_frame(value):
        value = value.reshape(groups, 2 * frames_dev, GROUP, value.shape[-1]).transpose(1, 0, 2, 3)
        return value.reshape(2, frames_dev, span, value.shape[-1])

    def cut(value, x_place, y_place):
        start = (x_place * 4 + y_place * 2 + c_me) * span
        return lax.dynamic_slice_in_dim(value, start, span, axis=1)

    keep_own = keep_of(wide_me)
    keep_far = keep_of(wide_me + 1 - 2 * x_me)
    keep_place = jnp.broadcast_to(
        jnp.concatenate([keep_own, keep_far])[None, :, None], (groups, 2 * frames_dev, GROUP)
    ).reshape(rows, 1)
    choose = (
        actions[:, None] == jnp.arange(action_table.shape[0], dtype=jnp.int32)[None, :]
    ).astype(BF16)
    extra = jnp.dot(choose, action_table, preferred_element_type=F32)

    far_tokens = swap(cut(tokens, 1 - x_me, y_me), "wide", 1)
    far_extra = swap(extra.astype(BF16), "wide", 1).astype(F32)
    merge1_all = gather_narrow(spatial_merge)
    project_all = gather_narrow(temporal_project)
    merge2_all = gather_narrow(temporal_merge)

    normed1, heads1, mixed1 = spatial_forward(tokens, extra, norm_gains[0:1], spatial_project)

    shaped = mixed1.reshape(frames_dev, 2, tokens_frame // 2, local)
    moved = jnp.stack([pick(shaped, x_me, 1), swap(pick(shaped, 1 - x_me, 1), "wide", 1)])
    moved = moved.reshape(2, frames_dev, 2, tokens_frame // 4, local)
    moved = jnp.stack([pick(moved, y_me, 2), swap(pick(moved, 1 - y_me, 2), "narrow", 2)])
    moved = moved.reshape(2, 2, frames_dev, 2, span, local)
    moved = jnp.stack([pick(moved, c_me, 3), swap(pick(moved, 1 - c_me, 3), "narrow", 1)], axis=1)
    mixed1_all = moved.reshape(4, 2 * frames_dev, groups, GROUP, local).transpose(0, 2, 1, 3, 4)
    mixed1_all = mixed1_all.reshape(4, rows, local)

    expand_pair = jnp.stack([expand_weight, swap(after(expand_weight, mixed1), "narrow", 1)])
    reduce_pair = jnp.stack([reduce_weight, swap(after(reduce_weight, mixed1), "narrow", 1)])
    grad_far = swap(
        after(
            jnp.stack([cut(grad_out, 1 - x_me, y_me), cut(grad_out, 1 - x_me, 1 - y_me)]), mixed1_all
        ),
        "wide",
        1,
    )

    start_place = by_place(
        cut(tokens, x_me, y_me).astype(F32) + extra[:, None, :],
        far_tokens.astype(F32) + far_extra[:, None, :],
    )
    hidden1, normed2, heads2, mixed2, hidden2, normed3 = temporal_forward(
        start_place, keep_place, norm_gains, mixed1_all, merge1_all, project_all, merge2_all
    )

    grad_result = by_place(cut(grad_out, x_me, y_me), grad_far[0])
    grad_result_far = by_place(cut(grad_out, x_me, 1 - y_me), grad_far[1])
    normed3_far = swap(normed3, "narrow", 2)
    near = feed_forward(normed3, grad_result, keep_place, expand_pair, reduce_pair)
    far = feed_forward(normed3_far, grad_result_far, keep_place, expand_pair, reduce_pair)
    grad_normed3_far = swap(far[4], "narrow", 2)
    units = expand_weight.shape[1]
    per = units // 256
    reduce_grad = outer(
        [(near[0], near[2]), (far[0], far[2])],
        (2 * per,),
        lambda j: (0, j),
        lambda j: (0, 0),
        lambda j: (j // per, j % per, 0),
        (rows, 256),
        (rows, width),
        (2, units, width),
        2 * 2 * rows * 2 * units * width,
    )
    expand_grad = outer(
        [(normed3, near[1]), (normed3_far, far[1])],
        (2, width // 256),
        lambda c, j: (0, j),
        lambda c, j: (0, c),
        lambda c, j: (c, j, 0),
        (rows, 256),
        (rows, units),
        (2, width, units),
        2 * 2 * rows * 2 * units * width,
    )

    branch2_grad, grad_heads2, branch1_grad, grad_mixed1, carried, gain_three, gain_two = temporal_backward(
        near[4],
        grad_normed3_far,
        hidden2,
        hidden1,
        grad_result,
        keep_place,
        norm_gains,
        heads2,
        merge2_all,
        project_all,
        merge1_all,
    )

    moved = grad_mixed1.reshape(2, 2, groups, 2, frames_dev, GROUP, local)
    moved = moved.transpose(0, 1, 3, 4, 2, 5, 6).reshape(2, 2, 2, frames_dev, span, local)
    near_part, other = moved[:, 0], swap(moved[:, 1], "narrow", 1)
    moved = jnp.stack(
        [jnp.where(c_me == 0, near_part, other), jnp.where(c_me == 0, other, near_part)], axis=3
    )
    near_part, other = moved[0], swap(moved[1], "narrow", 2)
    moved = jnp.stack(
        [jnp.where(y_me == 0, near_part, other), jnp.where(y_me == 0, other, near_part)], axis=2
    )
    near_part, other = moved[0], swap(moved[1], "wide", 1)
    moved = jnp.stack(
        [jnp.where(x_me == 0, near_part, other), jnp.where(x_me == 0, other, near_part)], axis=1
    )
    grad_mixed1 = moved.reshape(frames_dev, tokens_frame, local)

    hidden_parts = by_frame(carried)
    grad_hidden_own = jnp.stack([hidden_parts[0], swap(hidden_parts[1], "wide", 1)], axis=1)

    branch3 = near[3].astype(F32) + swap(after(far[3], grad_normed3_far), "narrow", 2).astype(F32)
    result = (hidden2 + keep_place * branch3).astype(BF16)
    result = after(by_frame(result), grad_mixed1)
    result = jnp.stack([result[0], swap(result[1], "wide", 1)])
    result = jnp.stack([result, swap(result, "narrow", 2)])
    result = jnp.stack([result, swap(result, "narrow", 1)])
    output = in_order(result, BF16)

    grad_heads1, partial = spatial_backward(heads1, grad_mixed1, spatial_project)
    partial = partial.reshape(frames_dev, 2, 2, 2, span, width)
    partial = halve(partial, 3, "narrow", 1, c_me)
    partial = halve(partial, 2, "narrow", 2, y_me)
    grad_normed1 = jnp.stack([pick(partial, x_me, 1), pick(partial, 1 - x_me, 1)], axis=1).astype(F32)
    start_own = (
        jnp.stack([cut(tokens, x_me, y_me), cut(tokens, 1 - x_me, y_me)], axis=1).astype(F32)
        + extra[:, None, None, :]
    )
    flat = (2 * frames_dev * span, width)
    back_one, gain_one = norm_back(start_own.reshape(flat), norm_gains[0:1], grad_normed1.reshape(flat))
    grad_start = grad_hidden_own.astype(F32) + back_one.reshape(grad_hidden_own.shape)
    frame_totals = jnp.sum(grad_start, axis=(1, 2))
    table_grad = jnp.dot(choose.astype(F32).T, frame_totals, precision=HIGHEST)
    grad_part = grad_start.astype(BF16).transpose(1, 0, 2, 3)
    grad_part = jnp.stack([grad_part, swap(grad_part, "narrow", 2)])
    grad_part = jnp.stack([grad_part, swap(grad_part, "narrow", 1)])
    grad_tokens = in_order(grad_part, F32)

    small = jnp.concatenate([gain_one, gain_two, gain_three, table_grad])
    small = small + swap(small, "narrow", 1)
    small = small + swap(small, "narrow", 2)
    wide = lax.axis_size("wide")
    bit = 1
    while bit < wide:
        small = small + swap(small, "wide", bit)
        bit *= 2
    small = lax.dynamic_slice_in_dim(small, wide_me * (width // wide), width // wide, axis=1)

    reduce_grad = after(reduce_grad, grad_mixed1)
    expand_grad = after(expand_grad, grad_mixed1)
    reduce_grad = added(reduce_grad[0], swap(reduce_grad[1], "narrow", 1))
    expand_grad = added(expand_grad[0], swap(expand_grad[1], "narrow", 1))
    reduce_out = scatter_wide(reduce_grad, 1).astype(F32)
    expand_out = scatter_wide(expand_grad, 0).astype(F32)

    def merge_grad(mixed, grad):
        return outer(
            [(mixed, grad)],
            (4,),
            lambda n: (n, 0, 0),
            lambda n: (0, 0),
            lambda n: (n, 0, 0),
            (1, rows, local),
            (rows, width),
            (4, local, width),
            2 * rows * width * width,
        )

    merge2_grad = merge_grad(mixed2, branch2_grad)
    merge1_grad = merge_grad(mixed1_all, branch1_grad)
    project2_grad = outer(
        [(normed2, grad_heads2)],
        (4, 3),
        lambda n, c: (0, 0),
        lambda n, c: (n, c, 0, 0),
        lambda n, c: (n, c, 0, 0),
        (rows, width),
        (1, 1, rows, local),
        (4, 3, width, local),
        6 * rows * width * width,
    )
    all_rows = frames_dev * tokens_frame
    project1_grad = outer(
        [(normed1.reshape(all_rows, width), grad_heads1.reshape(3, all_rows, local))],
        (3, width // 256),
        lambda c, j: (0, j),
        lambda c, j: (c, 0, 0),
        lambda c, j: (c, j, 0),
        (all_rows, 256),
        (1, all_rows, local),
        (3, width, local),
        6 * all_rows * width * local,
    )
    project2_out = scatter_wide(scatter_narrow(project2_grad), 1).astype(F32).transpose(1, 0, 2)
    merge2_out = scatter_wide(scatter_narrow(merge2_grad), 1).astype(F32)
    merge1_out = scatter_wide(scatter_narrow(merge1_grad), 1).astype(F32)
    project1_out = scatter_wide(project1_grad, 1).astype(F32).transpose(1, 0, 2)
    return (
        output,
        grad_tokens,
        small[:3],
        small[3:],
        project1_out,
        merge1_out,
        project2_out,
        merge2_out,
        expand_out,
        reduce_out,
    )


def solution(mesh):
    return jax.shard_map(
        body,
        mesh=mesh,
        in_specs=(
            P("wide", None, None),
            P(),
            P("wide"),
            P(),
            P(),
            P(None, None, "narrow"),
            P("narrow", None),
            P(None, None, "narrow"),
            P("narrow", None),
            P(None, "narrow"),
            P("narrow", None),
            P("wide", None, None),
        ),
        out_specs=(
            P("wide", None, None),
            P("wide", None, None),
            P(None, "wide"),
            P(None, "wide"),
            P("wide", None, "narrow"),
            P("narrow", "wide"),
            P("wide", None, "narrow"),
            P("narrow", "wide"),
            P("wide", "narrow"),
            P("narrow", "wide"),
        ),
        check_vma=False,
    )
```

time: 786 us -> 645 us (0.82)
  the two profiles are of different devices: /device:TPU:31 before, /device:TPU:0 now
where the time goes in v2:
time: 645 us; the launch traced here: 633 us
  waiting for transfers between devices  222 us (34%)
  Pallas kernels  192 us (30%)
  other arithmetic  80.8 us (13%)
  starting transfers between devices  68.7 us (11%)
  local copies, waits for them, and re-layouts  67.2 us (10%)
    ppermute x59, waiting for transfers between devices, swap(): return lax.ppermute(value, axis, [(i, i ^ bit) for i in range(size)])  222 us
    ppermute x59, starting transfers between devices, swap(): return lax.ppermute(value, axis, [(i, i ^ bit) for i in range(size)])  68.7 us
    pallas_call x6, Pallas kernels, outer(): call(kernel, blocks, specs, pl.BlockSpec(out_block, out_map), shape_of(ou...  55.6 us
    pallas_call x1, Pallas kernels, temporal_backward(): call(kernel, (4,), [full, full, full, full, full, whole((rows, 1)), whole...  31.6 us
    pallas_call x2, Pallas kernels, feed_forward(): call(kernel, (cores * per,), [full, full, whole((rows, 1)), pl.BlockSpec(...  30.1 us
    convert_element_type x22, other arithmetic, added(): return (left.astype(F32) + right.astype(F32)).astype(BF16)  22.7 us
    pallas_call x1, Pallas kernels, temporal_forward(): call(kernel, (4,), [whole((rows, width)), whole((rows, 1)), whole((3, wid...  21.9 us
    pallas_call x1, Pallas kernels, spatial_backward(): call(kernel, (frames,), [pl.BlockSpec((3, 1, places, local), lambda f: (0...  21 us
  transfers between devices with their start and end apart: 59, of which 22 were waited for; matrix products, arithmetic and copies ran while one was open for 22% of the time, Pallas kernels for 27%

profile of v2, /device:TPU:0, one launch (start us, length us, event | category | flops | bytes accessed | tf_op | source)
XLA Modules:
  0.0 633.4 jit_solution(14883841367787938314)
XLA Ops:
  0.7 3.0 collective-permute-start.7
  8.7 16.7 %shard_map.195 = (bf16[8,256,1024]{2,1,0:T(8,128)(2,1)}, bf16[3,8,256,256]{3,2,1,0:T(8,128)(2,1)}, bf16[8,256,256]{2,1,0:T(8,128)(2,1)}) custom-call(bf16[8,256,1024]{2,1,0:T(8,128)(2,1)} %tokens_ref.1, f32[8,1,1024]{2,1,0:T(1,128)} %broadcast_in_dim.25.extra_ref, f32[1,1024]{1,0:T(1,128)} %slice.114.gain_ref, bf16[3,1024,256]{2,1,0:T(8,128)(2,1)} %bitcast.365), custom_call_target="tpu_custom_call" | custom-call | flops 4294967296 | bytes 12582912 | tf_op jit(solution)/shard_map/pallas_call | solution.py:119
  25.4 2.4 dynamic-slice_bitcast_fusion.8
  30.7 2.2 convert_add_fusion.15
  32.9 6.3 %collective-permute-done.7 = bf16[3,1024,256]{2,1,0:T(8,128)(2,1)} collective-permute-done((bf16[3,1024,256]{2,1,0:T(8,128)(2,1)}, bf16[3,1024,256]{2,1,0:T(8,128)(2,1)}, u32[]{:S(2)}, u32[]{:S(2)}) %collective-permute-start.7) | collective-permute-done | bytes 1572896 | tf_op jit(solution)/shard_map/ppermute | solution.py:530
  39.2 3.4 pad_maximum_fusion.5
  43.6 2.1 fusion.31
  45.7 2.1 collective-permute-start.3
  51.9 2.8 constant_dynamic-slice_fusion.18
  54.6 7.1 %collective-permute-done.9 = bf16[256,1024]{1,0:T(8,128)(2,1)} collective-permute-done((bf16[256,1024]{1,0:T(8,128)(2,1)}, bf16[256,1024]{1,0:T(8,128)(2,1)}, u32[]{:S(2)}, u32[]{:S(2)}) %collective-permute-start.9) | collective-permute-done | bytes 524320 | tf_op jit(solution)/shard_map/ppermute | solution.py:530
  61.7 2.0 collective-permute-start.1
  65.0 7.1 %collective-permute-done.3 = bf16[2,8,64,256]{3,2,1,0:T(8,128)(2,1)} collective-permute-done((bf16[2,8,64,256]{3,2,1,0:T(8,128)(2,1)}, bf16[2,8,64,256]{3,2,1,0:T(8,128)(2,1)}, u32[]{:S(2)}, u32[]{:S(2)}) %collective-permute-start.3) | collective-permute-done | bytes 524320 | tf_op jit(solution)/shard_map/ppermute | solution.py:530
  82.5 2.8 pad_maximum_fusion.7.merge1_ref
  85.3 2.8 pad_maximum_fusion.8.merge2_ref
  88.1 2.1 fusion.63
  90.2 4.3 pad_maximum_fusion.project_ref
  94.5 21.9 %shard_map.196 = (f32[512,1024]{1,0:T(8,128)}, bf16[512,1024]{1,0:T(8,128)(2,1)}, bf16[4,3,512,256]{3,2,1,0:T(8,128)(2,1)}, bf16[4,512,256]{2,1,0:T(8,128)(2,1)}...) custom-call(f32[512,1024]{1,0:T(8,128)} %bitcast.332, f32[512,1]{1,0:T(8,128)} %reshape.358.keep_ref, ...), custom_call_target="tpu_custom_call" | custom-call | flops 6442450944 | bytes 25165824 | tf_op jit(solution)/shard_map/pallas_call | solution.py:206
  118.6 4.0 pad_maximum_fusion.1.expand_ref
  122.6 4.0 pad_maximum_fusion.2.reduce_ref
  130.4 11.1 %collective-permute-done.14.normed_ref.refs_2_ = bf16[512,1024]{1,0:T(8,128)(2,1)S(1)} collective-permute-done((bf16[512,1024]{1,0:T(8,128)(2,1)}, bf16[512,1024]{1,0:T(8,128)(2,1)S(1)}, u32[]{:S(2)}, u32[]{:S(2)}) %collective-permute-start.14) | collective-permute-done | bytes 1048608 | tf_op jit(solution)/shard_map/ppermute | solution.py:530
  142.5 15.1 %shard_map.198 = (bf16[512,2048]{1,0:T(8,128)(2,1)}, bf16[512,2048]{1,0:T(8,128)(2,1)}, bf16[512,1024]{1,0:T(8,128)(2,1)}, bf16[512,1024]{1,0:T(8,128)(2,1)}, bf16[512,1024]{1,0:T(8,128)(2,1)}) custom-call(bf16[512,1024]{1,0:T(8,128)(2,1)} %copy-done.38, bf16[512,1024]{1,0:T(8,128)(2,1)} %bitcast.348, f32[512,1]{1,0:T(8,128)} %reshape.358.keep_ref, ...), custom_call_target="tpu_custom_call" | custom-call | flops 8589934592 | bytes 18874368 | tf_op jit(solution)/shard_map/pallas_call | solution.py:290
  159.2 15.0 %shard_map.197 = (bf16[512,2048]{1,0:T(8,128)(2,1)}, bf16[512,2048]{1,0:T(8,128)(2,1)}, bf16[512,1024]{1,0:T(8,128)(2,1)}, bf16[512,1024]{1,0:T(8,128)(2,1)}, bf16[512,1024]{1,0:T(8,128)(2,1)}) custom-call(bf16[512,1024]{1,0:T(8,128)(2,1)} %get-tuple-element.47.normed_ref.refs_0_, bf16[512,1024]{1,0:T(8,128)(2,1)} %bitcast.345, f32[512,1]{1,0:T(8,128)} %reshape.358.keep_ref, ...), custom_call_target="tpu_custom_call" | custom-call | flops 8589934592 | bytes 18874368 | tf_op jit(solution)/shard_map/pallas_call | solution.py:290
  174.2 10.1 %shard_map.208 = bf16[2,1024,1024]{2,1,0:T(8,128)(2,1)} custom-call(bf16[512,2048]{1,0:T(8,128)(2,1)} %get-tuple-element.75.refs_0_, bf16[512,1024]{1,0:T(8,128)(2,1)} %get-tuple-element.76.refs_1_, bf16[512,2048]{1,0:T(8,128)(2,1)} %get-tuple-element.77.refs_2_, bf16[512,1024]{1,0:T(8,128)(2,1)} %get-tuple-element.78.refs_3_), custom_call_target="tpu_custom_call" | custom-call | flops 4294967296 | bytes 16777216 | tf_op jit(solution)/shard_map/pallas_call | solution.py:335
  184.3 10.8 %shard_map.207 = bf16[2,1024,1024]{2,1,0:T(8,128)(2,1)} custom-call(bf16[512,1024]{1,0:T(8,128)(2,1)} %get-tuple-element.47.normed_ref.refs_0_, bf16[512,2048]{1,0:T(8,128)(2,1)} %get-tuple-element.72.refs_1_, bf16[512,1024]{1,0:T(8,128)(2,1)} %copy-done.38, bf16[512,2048]{1,0:T(8,128)(2,1)} %get-tuple-element.73.refs_3_), custom_call_target="tpu_custom_call" | custom-call | flops 4294967296 | bytes 16777216 | tf_op jit(solution)/shard_map/pallas_call | solution.py:335
  196.1 31.6 %shard_map.199 = (bf16[512,1024]{1,0:T(8,128)(2,1)}, bf16[4,3,512,256]{3,2,1,0:T(8,128)(2,1)}, bf16[512,1024]{1,0:T(8,128)(2,1)}, bf16[4,512,256]{2,1,0:T(8,128)...) custom-call(bf16[512,1024]{1,0:T(8,128)(2,1)} %get-tuple-element.55.near_ref, ...), custom_call_target="tpu_custom_call" | custom-call | flops 8589934592 | bytes 31457280 | tf_op jit(solution)/shard_map/pallas_call | solution.py:418
  230.1 4.8 shard_map.204
  237.4 11.6 %shard_map.205 = bf16[4,3,1024,256]{3,2,1,0:T(8,128)(2,1)} custom-call(bf16[512,1024]{1,0:T(8,128)(2,1)} %get-tuple-element.68.refs_0_, bf16[4,3,512,256]{3,2,1,0:T(8,128)(2,1)} %get-tuple-element.69.refs_1_), custom_call_target="tpu_custom_call" | custom-call | flops 3221225472 | bytes 16777216 | tf_op jit(solution)/shard_map/pallas_call | solution.py:335
  249.0 3.8 slice.174
  253.7 5.0 shard_map.206
  268.2 83.9 %collective-permute-done.46 = bf16[2,256,1024]{2,1,0:T(8,128)(2,1)S(1)} collective-permute-done((bf16[2,256,1024]{2,1,0:T(8,128)(2,1)S(1)}, bf16[2,256,1024]{2,1,0:T(8,128)(2,1)S(1)}, u32[]{:S(2)}, u32[]{:S(2)}) %collective-permute-start.46) | collective-permute-done | bytes 1048608 | tf_op jit(solution)/shard_map/ppermute | solution.py:530
  353.4 9.5 %collective-permute-done.18 = bf16[2,8,2,32,256]{4,3,2,1,0:T(8,128)(2,1)S(1)} collective-permute-done((bf16[2,8,2,32,256]{4,3,2,1,0:T(8,128)(2,1)S(1)}, bf16[2,8,2,32,256]{4,3,2,1,0:T(8,128)(2,1)S(1)}, u32[]{:S(2)}, u32[]{:S(2)}) %collective-permute-start.18) | collective-permute-done | bytes 524320 | tf_op jit(solution)/shard_map/ppermute | solution.py:530
  375.2 3.9 collective-permute-done.19
  382.8 21.0 %shard_map.201 = (bf16[3,8,256,256]{3,2,1,0:T(8,128)(2,1)}, bf16[8,256,1024]{2,1,0:T(8,128)(2,1)}) custom-call(bf16[3,8,256,256]{3,2,1,0:T(8,128)(2,1)} %get-tuple-element.61.heads_ref, bf16[8,256,256]{2,1,0:T(8,128)(2,1)} %bitcast.350, bf16[3,1024,256]{2,1,0:T(8,128)(2,1)} %bitcast.366), custom_call_target="tpu_custom_call" | custom-call | flops 5368709120 | bytes 14680064 | tf_op jit(solution)/shard_map/pallas_call | solution.py:483
  403.7 2.8 constant_dynamic-slice_fusion.16
  412.7 13.2 %shard_map.203 = bf16[3,1024,256]{2,1,0:T(8,128)(2,1)} custom-call(bf16[2048,1024]{1,0:T(8,128)(2,1)} %bitcast.367, bf16[3,2048,256]{2,1,0:T(8,128)(2,1)} %bitcast.368), custom_call_target="tpu_custom_call" | custom-call | flops 3221225472 | bytes 16777216 | tf_op jit(solution)/shard_map/pallas_call | solution.py:335
  432.6 2.4 collective-permute-done.39
  436.6 3.3 collective-permute-done.49
  440.0 3.1 collective-permute-start.40
  443.1 2.8 collective-permute-done.33
  449.7 2.6 collective-permute-start.50
  453.6 4.2 collective-permute-done.34
  461.8 6.1 collective-permute-done.35
  470.2 2.8 add_convert_fusion
  474.4 4.6 collective-permute-done.21
  479.0 2.3 fusion.60
  481.8 2.8 fusion.2
  490.9 2.3 fusion
  493.3 3.5 reshape.332
  496.7 4.3 constant_dynamic-slice_fusion.2
  504.9 6.7 %collective-permute-done.25 = bf16[8,2,32,1024]{3,2,0,1:T(8,128)(2,1)} collective-permute-done((bf16[8,2,32,1024]{3,2,0,1:T(8,128)(2,1)}, bf16[8,2,32,1024]{3,2,0,1:T(8,128)(2,1)}, u32[]{:S(2)}, u32[]{:S(2)}) %collective-permute-start.25) | collective-permute-done | bytes 1048608 | tf_op jit(solution)/shard_map/ppermute | solution.py:530
  523.0 22.9 %collective-permute-done.29 = f32[11,1024]{1,0:T(8,128)S(1)} collective-permute-done((f32[11,1024]{1,0:T(8,128)S(1)}, f32[11,1024]{1,0:T(8,128)S(1)}, u32[]{:S(2)}, u32[]{:S(2)}) %collective-permute-start.29) | collective-permute-done | bytes 45088 | tf_op jit(solution)/shard_map/ppermute | solution.py:530
  546.5 8.6 %collective-permute-done.30 = f32[11,1024]{1,0:T(8,128)S(1)} collective-permute-done((f32[11,1024]{1,0:T(8,128)S(1)}, f32[11,1024]{1,0:T(8,128)S(1)}, u32[]{:S(2)}, u32[]{:S(2)}) %collective-permute-start.30) | collective-permute-done | bytes 45088 | tf_op jit(solution)/shard_map/ppermute | solution.py:530
  557.5 11.8 %collective-permute-done.31 = f32[11,1024]{1,0:T(8,128)S(1)} collective-permute-done((f32[11,1024]{1,0:T(8,128)S(1)}, f32[11,1024]{1,0:T(8,128)S(1)}, u32[]{:S(2)}, u32[]{:S(2)}) %collective-permute-start.31) | collective-permute-done | bytes 45088 | tf_op jit(solution)/shard_map/ppermute | solution.py:530
  569.3 3.6 collective-permute-start.32
  572.9 2.2 collective-permute-done.32
  578.7 3.5 collective-permute-start.54
  582.2 8.3 %collective-permute-done.57 = bf16[1024,2,128]{2,0,1:T(8,128)(2,1)S(1)} collective-permute-done((bf16[1024,2,128]{2,0,1:T(8,128)(2,1)S(1)}, bf16[1024,2,128]{2,0,1:T(8,128)(2,1)S(1)}, u32[]{:S(2)}, u32[]{:S(2)}) %collective-permute-start.57) | collective-permute-done | bytes 524320 | tf_op jit(solution)/shard_map/ppermute | solution.py:530
  590.7 5.0 collective-permute-start.58
  596.0 2.5 collective-permute-start.44
  598.6 4.0 pad_maximum_fusion.3.value_ref
  602.5 7.3 %shard_map.200 = bf16[8,256,1024]{2,1,0:T(8,128)(2,1)} custom-call(s32[3]{0:T(128)} %pad_add_fusion.me_ref, bf16[2,2,2,8,32,1024]{5,4,3,2,1,0:T(8,128)(2,1)} %pad_maximum_fusion.3.value_ref), custom_call_target="tpu_custom_call" | custom-call | bytes 12582912 | tf_op jit(solution)/shard_map/pallas_call | solution.py:509
  613.7 6.3 collective-permute-done.45
  620.8 4.0 pad_maximum_fusion.4.value_ref
  624.8 8.1 %shard_map.202 = f32[8,256,1024]{2,1,0:T(8,128)} custom-call(s32[3]{0:T(128)} %pad_add_fusion.me_ref, bf16[2,2,2,8,32,1024]{5,4,3,2,1,0:T(8,128)(2,1)} %pad_maximum_fusion.4.value_ref), custom_call_target="tpu_custom_call" | custom-call | bytes 12582912 | tf_op jit(solution)/shard_map/pallas_call | solution.py:509
  (291 shorter events, 127.0 us)
Async XLA Ops:
  0.7 38.6 %collective-permute-start.7 = (bf16[3,1024,256]{2,1,0:T(8,128)(2,1)}, bf16[3,1024,256]{2,1,0:T(8,128)(2,1)}, u32[]{:S(2)}, u32[]{:S(2)}) collective-permute-start(bf16[3,1024,256]{2,1,0:T(8,128)(2,1)} %bitcast.308), channel_id=1, source_target_pairs={{0,2},{1,3},{2,0},{3,1},{4,6},{5,7},{6,4},{7,5},{8,10},{9,11},{10,... | collective-permute-start | bytes 4718600 | tf_op jit(solution)/shard_map/ppermute | solution.py:530
  5.0 70.1 %collective-permute-start = (bf16[8,32,1024]{2,1,0:T(8,128)(2,1)S(1)}, bf16[8,32,1024]{2,1,0:T(8,128)(2,1)}, u32[]{:S(2)}, u32[]{:S(2)}) collective-permute-start(bf16[8,32,1024]{2,1,0:T(8,128)(2,1)S(1)} %get-tuple-element.89), channel_id=1, source_target_pairs={{0,4},{4,0},{8,12},{12,8},{16,20},{20,16},{24,28},{28,24},{1,5},{5... | collective-permute-start | bytes 1572872 | tf_op jit(solution)/shard_map/ppermute | solution.py:530
  27.8 15.0 %collective-permute-start.2 = (bf16[8,128,256]{2,1,0:T(8,128)(2,1)}, bf16[8,128,256]{2,1,0:T(8,128)(2,1)S(1)}, u32[]{:S(2)}, u32[]{:S(2)}) collective-permute-start(bf16[8,128,256]{2,1,0:T(8,128)(2,1)} %get-tuple-element.128), channel_id=1, source_target_pairs={{0,4},{4,0},{8,12},{12,8},{16,20},{20,16},{24,28},{28,24},{1,5},{5... | collective-permute-start | bytes 1572872 | tf_op jit(solution)/shard_map/ppermute | solution.py:530
  28.3 22.2 %collective-permute-start.5 = (bf16[256,1024]{1,0:T(8,128)(2,1)}, bf16[256,1024]{1,0:T(8,128)(2,1)}, u32[]{:S(2)}, u32[]{:S(2)}) collective-permute-start(bf16[256,1024]{1,0:T(8,128)(2,1)} %param.18), channel_id=1, source_target_pairs={{0,2},{1,3},{2,0},{3,1},{4,6},{5,7},{6,4},{7,5},{8,10},{9,11},{10,... | collective-permute-start | bytes 1572872 | tf_op jit(solution)/shard_map/ppermute | solution.py:530
  28.4 33.3 %collective-permute-start.9 = (bf16[256,1024]{1,0:T(8,128)(2,1)}, bf16[256,1024]{1,0:T(8,128)(2,1)}, u32[]{:S(2)}, u32[]{:S(2)}) collective-permute-start(bf16[256,1024]{1,0:T(8,128)(2,1)} %param.20), channel_id=1, source_target_pairs={{0,2},{1,3},{2,0},{3,1},{4,6},{5,7},{6,4},{7,5},{8,10},{9,11},{10,... | collective-permute-start | bytes 1572872 | tf_op jit(solution)/shard_map/ppermute | solution.py:530
  42.6 45.5 %collective-permute-start.8 = (bf16[2,3,1024,256]{3,2,1,0:T(8,128)(2,1)}, bf16[2,3,1024,256]{3,2,1,0:T(8,128)(2,1)}, u32[]{:S(2)}, u32[]{:S(2)}) collective-permute-start(bf16[2,3,1024,256]{3,2,1,0:T(8,128)(2,1)} %pad_maximum_fusion.5), channel_id=1, source_target_pairs={{0,1},{1,0},{2,3},{3,2},{4,5},{5,4},{6,7},{7,6},{8,9},{9,8},{10,11... | collective-permute-start | bytes 9437192 | tf_op jit(solution)/shard_map/ppermute | solution.py:530
  45.7 26.4 %collective-permute-start.3 = (bf16[2,8,64,256]{3,2,1,0:T(8,128)(2,1)}, bf16[2,8,64,256]{3,2,1,0:T(8,128)(2,1)}, u32[]{:S(2)}, u32[]{:S(2)}) collective-permute-start(bf16[2,8,64,256]{3,2,1,0:T(8,128)(2,1)} %get-tuple-element.126), channel_id=1, source_target_pairs={{0,2},{1,3},{2,0},{3,1},{4,6},{5,7},{6,4},{7,5},{8,10},{9,11},{10,... | collective-permute-start | bytes 1572872 | tf_op jit(solution)/shard_map/ppermute | solution.py:530
  51.8 28.8 %collective-permute-start.6 = (bf16[2,256,1024]{2,1,0:T(8,128)(2,1)S(1)}, bf16[2,256,1024]{2,1,0:T(8,128)(2,1)S(1)}, u32[]{:S(2)}, u32[]{:S(2)}) collective-permute-start(bf16[2,256,1024]{2,1,0:T(8,128)(2,1)S(1)} %pad_maximum_fusion.12), channel_id=1, source_target_pairs={{0,1},{1,0},{2,3},{3,2},{4,5},{5,4},{6,7},{7,6},{8,9},{9,8},{10,11... | collective-permute-start | bytes 3145736 | tf_op jit(solution)/shard_map/ppermute | solution.py:530
  61.7 11.7 %collective-permute-start.1 = (bf16[8,1024]{1,0:T(8,128)(2,1)S(1)}, bf16[8,1024]{1,0:T(8,128)(2,1)S(1)}, u32[]{:S(2)}, u32[]{:S(2)}) collective-permute-start(bf16[8,1024]{1,0:T(8,128)(2,1)S(1)} %get-tuple-element.134), channel_id=1, source_target_pairs={{0,4},{4,0},{8,12},{12,8},{16,20},{20,16},{24,28},{28,24},{1,5},{5... | collective-permute-start | bytes 49160 | tf_op jit(solution)/shard_map/ppermute | solution.py:530
  72.1 10.3 %collective-permute-start.10 = (bf16[2,256,1024]{2,1,0:T(8,128)(2,1)S(1)}, bf16[2,256,1024]{2,1,0:T(8,128)(2,1)S(1)}, u32[]{:S(2)}, u32[]{:S(2)}) collective-permute-start(bf16[2,256,1024]{2,1,0:T(8,128)(2,1)S(1)} %pad_maximum_fusion.13), channel_id=1, source_target_pairs={{0,1},{1,0},{2,3},{3,2},{4,5},{5,4},{6,7},{7,6},{8,9},{9,8},{10,11... | collective-permute-start | bytes 3145736 | tf_op jit(solution)/shard_map/ppermute | solution.py:530
  73.4 4.7 collective-permute-start.4
  75.1 43.5 %collective-permute-start.12 = (bf16[1024,1024]{1,0:T(8,128)(2,1)S(1)}, bf16[1024,1024]{1,0:T(8,128)(2,1)}, u32[]{:S(2)}, u32[]{:S(2)}) collective-permute-start(bf16[1024,1024]{1,0:T(8,128)(2,1)S(1)} %copy-done.25), channel_id=1, source_target_pairs={{0,1},{1,0},{2,3},{3,2},{4,5},{5,4},{6,7},{7,6},{8,9},{9,8},{10,11... | collective-permute-start | bytes 6291464 | tf_op jit(solution)/shard_map/ppermute | solution.py:530
  78.9 43.7 %collective-permute-start.13 = (bf16[1024,1024]{1,0:T(8,128)(2,1)S(1)}, bf16[1024,1024]{1,0:T(8,128)(2,1)}, u32[]{:S(2)}, u32[]{:S(2)}) collective-permute-start(bf16[1024,1024]{1,0:T(8,128)(2,1)S(1)} %copy-done.26), channel_id=1, source_target_pairs={{0,1},{1,0},{2,3},{3,2},{4,5},{5,4},{6,7},{7,6},{8,9},{9,8},{10,11... | collective-permute-start | bytes 6291464 | tf_op jit(solution)/shard_map/ppermute | solution.py:530
  80.6 46.0 %collective-permute-start.11 = (bf16[2,8,32,1024]{3,2,1,0:T(8,128)(2,1)}, bf16[2,8,32,1024]{3,2,1,0:T(8,128)(2,1)}, u32[]{:S(2)}, u32[]{:S(2)}) collective-permute-start(bf16[2,8,32,1024]{3,2,1,0:T(8,128)(2,1)} %pad_maximum_fusion.14), channel_id=1, source_target_pairs={{0,4},{4,0},{8,12},{12,8},{16,20},{20,16},{24,28},{28,24},{1,5},{5... | collective-permute-start | bytes 3145736 | tf_op jit(solution)/shard_map/ppermute | solution.py:530
  116.4 25.1 %collective-permute-start.14 = (bf16[512,1024]{1,0:T(8,128)(2,1)}, bf16[512,1024]{1,0:T(8,128)(2,1)S(1)}, u32[]{:S(2)}, u32[]{:S(2)}) collective-permute-start(bf16[512,1024]{1,0:T(8,128)(2,1)} %get-tuple-element.47.normed_ref.refs_0_), channel_id=1, source_target_pairs={{0,2},{1,3},{2,0},{3,1},{4,6},{5,7},{6,4},{7,5},{8,10},{9,11},{10,... | collective-permute-start | bytes 3145736 | tf_op jit(solution)/shard_map/ppermute | solution.py:530
  157.6 37.5 %collective-permute-start.15 = (bf16[512,1024]{1,0:T(8,128)(2,1)}, bf16[512,1024]{1,0:T(8,128)(2,1)S(1)}, u32[]{:S(2)}, u32[]{:S(2)}) collective-permute-start(bf16[512,1024]{1,0:T(8,128)(2,1)} %get-tuple-element.53), channel_id=1, source_target_pairs={{0,2},{1,3},{2,0},{3,1},{4,6},{5,7},{6,4},{7,5},{8,10},{9,11},{10,... | collective-permute-start | bytes 3145736 | tf_op jit(solution)/shard_map/ppermute | solution.py:530
  195.1 68.2 %collective-permute-start.16 = (bf16[512,1024]{1,0:T(8,128)(2,1)}, bf16[512,1024]{1,0:T(8,128)(2,1)S(1)}, u32[]{:S(2)}, u32[]{:S(2)}) collective-permute-start(bf16[512,1024]{1,0:T(8,128)(2,1)} %get-tuple-element.54), channel_id=1, source_target_pairs={{0,2},{1,3},{2,0},{3,1},{4,6},{5,7},{6,4},{7,5},{8,10},{9,11},{10,... | collective-permute-start | bytes 3145736 | tf_op jit(solution)/shard_map/ppermute | solution.py:530
  230.0 32.3 %collective-permute-start.17 = (bf16[2,2,8,32,256]{4,3,2,1,0:T(8,128)(2,1)}, bf16[2,2,8,32,256]{4,3,2,1,0:T(8,128)(2,1)S(1)}, u32[]{:S(2)}, u32[]{:S(2)}) collective-permute-start(bf16[2,2,8,32,256]{4,3,2,1,0:T(8,128)(2,1)} %slice_bitcast_fusion.8), channel_id=1, source_target_pairs={{0,1},{1,0},{2,3},{3,2},{4,5},{5,4},{6,7},{7,6},{8,9},{9,8},{10,11... | collective-permute-start | bytes 1572872 | tf_op jit(solution)/shard_map/ppermute | solution.py:530
  236.2 29.3 %collective-permute-start.36 = (bf16[2,256,1024]{2,1,0:T(8,128)(2,1)S(1)}, bf16[2,256,1024]{2,1,0:T(8,128)(2,1)}, u32[]{:S(2)}, u32[]{:S(2)}) collective-permute-start(bf16[2,256,1024]{2,1,0:T(8,128)(2,1)S(1)} %slice.170), channel_id=1, source_target_pairs={{0,2},{1,3},{2,0},{3,1},{4,6},{5,7},{6,4},{7,5},{8,10},{9,11},{10,... | collective-permute-start | bytes 3145736 | tf_op jit(solution)/shard_map/ppermute | solution.py:530
  252.8 215.9 %collective-permute-start.41 = (bf16[2,3,1024,256]{3,2,1,0:T(8,128)(2,1)}, bf16[2,3,1024,256]{3,2,1,0:T(8,128)(2,1)}, u32[]{:S(2)}, u32[]{:S(2)}) collective-permute-start(bf16[2,3,1024,256]{3,2,1,0:T(8,128)(2,1)} %slice.174), channel_id=1, source_target_pairs={{0,2},{1,3},{2,0},{3,1},{4,6},{5,7},{6,4},{7,5},{8,10},{9,11},{10,... | collective-permute-start | bytes 9437192 | tf_op jit(solution)/shard_map/ppermute | solution.py:530
  260.0 92.1 %collective-permute-start.46 = (bf16[2,256,1024]{2,1,0:T(8,128)(2,1)S(1)}, bf16[2,256,1024]{2,1,0:T(8,128)(2,1)S(1)}, u32[]{:S(2)}, u32[]{:S(2)}) collective-permute-start(bf16[2,256,1024]{2,1,0:T(8,128)(2,1)S(1)} %slice.178), channel_id=1, source_target_pairs={{0,2},{1,3},{2,0},{3,1},{4,6},{5,7},{6,4},{7,5},{8,10},{9,11},{10,... | collective-permute-start | bytes 3145736 | tf_op jit(solution)/shard_map/ppermute | solution.py:530
  262.4 100.6 %collective-permute-start.18 = (bf16[2,8,2,32,256]{4,3,2,1,0:T(8,128)(2,1)S(1)}, bf16[2,8,2,32,256]{4,3,2,1,0:T(8,128)(2,1)S(1)}, u32[]{:S(2)}, u32[]{:S(2)}) collective-permute-start(bf16[2,8,2,32,256]{4,3,2,1,0:T(8,128)(2,1)S(1)} %fusion.34), channel_id=1, source_target_pairs={{0,2},{1,3},{2,0},{3,1},{4,6},{5,7},{6,4},{7,5},{8,10},{9,11},{10,... | collective-permute-start | bytes 1572872 | tf_op jit(solution)/shard_map/ppermute | solution.py:530
  265.5 86.6 %copy-start.9 = (bf16[4,256,1024]{2,1,0:T(8,128)(2,1)S(1)}, bf16[4,256,1024]{2,1,0:T(8,128)(2,1)}, u32[]{:S(2)}) copy-start(bf16[4,256,1024]{2,1,0:T(8,128)(2,1)} %shard_map.206) | copy-start | bytes 6291460
  268.1 96.3 %collective-permute-start.37 = (bf16[256,1024]{1,0:T(8,128)(2,1)S(1)}, bf16[256,1024]{1,0:T(8,128)(2,1)S(1)}, u32[]{:S(2)}, u32[]{:S(2)}) collective-permute-start(bf16[256,1024]{1,0:T(8,128)(2,1)S(1)} %slice_bitcast_fusion.6), channel_id=1, source_target_pairs={{0,1},{1,0},{2,3},{3,2},{4,5},{5,4},{6,7},{7,6},{8,9},{9,8},{10,11... | collective-permute-start | bytes 1572872 | tf_op jit(solution)/shard_map/ppermute | solution.py:530
  353.4 16.9 %collective-permute-start.47 = (bf16[256,1024]{1,0:T(8,128)(2,1)}, bf16[256,1024]{1,0:T(8,128)(2,1)}, u32[]{:S(2)}, u32[]{:S(2)}) collective-permute-start(bf16[256,1024]{1,0:T(8,128)(2,1)} %slice_bitcast_fusion.4), channel_id=1, source_target_pairs={{0,1},{1,0},{2,3},{3,2},{4,5},{5,4},{6,7},{7,6},{8,9},{9,8},{10,11... | collective-permute-start | bytes 1572872 | tf_op jit(solution)/shard_map/ppermute | solution.py:530
  363.9 15.1 %collective-permute-start.19 = (bf16[8,2,2,32,256]{4,3,2,1,0:T(8,128)(2,1)}, bf16[8,2,2,32,256]{4,3,2,1,0:T(8,128)(2,1)}, u32[]{:S(2)}, u32[]{:S(2)}) collective-permute-start(bf16[8,2,2,32,256]{4,3,2,1,0:T(8,128)(2,1)} %fusion.33), channel_id=1, source_target_pairs={{0,4},{4,0},{8,12},{12,8},{16,20},{20,16},{24,28},{28,24},{1,5},{5... | collective-permute-start | bytes 1572872 | tf_op jit(solution)/shard_map/ppermute | solution.py:530
  368.8 58.6 %collective-permute-start.38 = (bf16[256,4,128]{2,0,1:T(8,128)(2,1)S(1)}, bf16[256,4,128]{2,0,1:T(8,128)(2,1)}, u32[]{:S(2)}, u32[]{:S(2)}) collective-permute-start(bf16[256,4,128]{2,0,1:T(8,128)(2,1)S(1)} %bitcast.360), channel_id=1, source_target_pairs={{0,4},{4,0},{8,12},{12,8},{16,20},{20,16},{24,28},{28,24},{1,5},{5... | collective-permute-start | bytes 786440 | tf_op jit(solution)/shard_map/ppermute | solution.py:530
  374.7 55.3 %collective-permute-start.48 = (bf16[256,4,128]{2,0,1:T(8,128)(2,1)}, bf16[256,4,128]{2,0,1:T(8,128)(2,1)}, u32[]{:S(2)}, u32[]{:S(2)}) collective-permute-start(bf16[256,4,128]{2,0,1:T(8,128)(2,1)} %bitcast.300), channel_id=1, source_target_pairs={{0,4},{4,0},{8,12},{12,8},{16,20},{20,16},{24,28},{28,24},{1,5},{5... | collective-permute-start | bytes 786440 | tf_op jit(solution)/shard_map/ppermute | solution.py:530
  382.3 67.4 %collective-permute-start.20 = (bf16[8,32,1024]{2,1,0:T(8,128)(2,1)}, bf16[8,32,1024]{2,1,0:T(8,128)(2,1)}, u32[]{:S(2)}, u32[]{:S(2)}) collective-permute-start(bf16[8,32,1024]{2,1,0:T(8,128)(2,1)} %get-tuple-element.117), channel_id=1, source_target_pairs={{0,4},{4,0},{8,12},{12,8},{16,20},{20,16},{24,28},{28,24},{1,5},{5... | collective-permute-start | bytes 1572872 | tf_op jit(solution)/shard_map/ppermute | solution.py:530
  408.2 73.1 %collective-permute-start.24 = (bf16[8,2,2,32,1024]{4,3,0,1,2:T(8,128)(2,1)}, bf16[8,2,2,32,1024]{4,3,0,1,2:T(8,128)(2,1)}, u32[]{:S(2)}, u32[]{:S(2)}) collective-permute-start(bf16[8,2,2,32,1024]{4,3,0,1,2:T(8,128)(2,1)} %bitcast.297), channel_id=1, source_target_pairs={{0,1},{1,0},{2,3},{3,2},{4,5},{5,4},{6,7},{7,6},{8,9},{9,8},{10,11... | collective-permute-start | bytes 6291464 | tf_op jit(solution)/shard_map/ppermute | solution.py:530
  412.7 16.2 %copy-start.23 = (bf16[256,4,1,128]{3,2,1,0:T(2,128)(2,1)S(1)}, bf16[256,4,1,128]{3,2,1,0:T(2,128)(2,1)}, u32[]{:S(2)}) copy-start(bf16[256,4,1,128]{3,2,1,0:T(2,128)(2,1)} %get-tuple-element.132) | copy-start | bytes 786436
  426.0 44.2 %slice-start = ((s8[6291456]{0:T(1024)(128)(4,1)}), s8[4194304]{0:T(1024)(128)(4,1)S(1)}, s32[]{:S(2)}) async-start(s8[6291456]{0:T(1024)(128)(4,1)} %bitcast.313), calls=%async_computation | async-start | bytes 8388608
  427.3 18.5 %collective-permute-start.33 = (bf16[3,4,128,256]{3,2,1,0:T(8,128)(2,1)S(1)}, bf16[3,4,128,256]{3,2,1,0:T(8,128)(2,1)S(1)}, u32[]{:S(2)}, u32[]{:S(2)}) collective-permute-start(bf16[3,4,128,256]{3,2,1,0:T(8,128)(2,1)S(1)} %dynamic-slice_bitcast_fusion.3), channel_id=1, source_target_pairs={{0,4},{4,0},{8,12},{12,8},{16,20},{20,16},{24,28},{28,24},{1,5},{5... | collective-permute-start | bytes 2359304 | tf_op jit(solution)/shard_map/ppermute | solution.py:530
  430.0 5.0 collective-permute-start.39
  432.6 16.3 %copy-start.21 = (bf16[1024,1024]{1,0:T(8,128)(2,1)S(1)}, bf16[1024,1024]{1,0:T(8,128)(2,1)}, u32[]{:S(2)}) copy-start(bf16[1024,1024]{1,0:T(8,128)(2,1)} %slice_bitcast_fusion.1) | copy-start | bytes 6291460
  435.0 5.0 collective-permute-start.49
  440.0 9.0 %collective-permute-start.40 = (bf16[256,1,128]{2,0,1:T(8,128)(2,1)S(1)}, bf16[256,1,128]{2,0,1:T(8,128)(2,1)S(1)}, u32[]{:S(2)}, u32[]{:S(2)}) collective-permute-start(bf16[256,1,128]{2,0,1:T(8,128)(2,1)S(1)} %constant_dynamic-slice_fusion.8), channel_id=1, source_target_pairs={{0,16},{4,20},{8,24},{12,28},{16,0},{20,4},{24,8},{28,12},{1,17},{... | collective-permute-start | bytes 196616 | tf_op jit(solution)/shard_map/ppermute | solution.py:530
  443.1 27.1 %slice-start.1 = ((s8[6291456]{0:T(1024)(128)(4,1)}), s8[2097152]{0:T(1024)(128)(4,1)S(1)}, s32[]{:S(2)}) async-start(s8[6291456]{0:T(1024)(128)(4,1)} %bitcast.313), calls=%async_computation.1 | async-start | bytes 4194304
  447.3 10.6 %collective-permute-start.34 = (bf16[3,2,128,256]{3,2,1,0:T(8,128)(2,1)S(1)}, bf16[3,2,128,256]{3,2,1,0:T(8,128)(2,1)S(1)}, u32[]{:S(2)}, u32[]{:S(2)}) collective-permute-start(bf16[3,2,128,256]{3,2,1,0:T(8,128)(2,1)S(1)} %dynamic-slice_bitcast_fusion.11), channel_id=1, source_target_pairs={{0,8},{4,12},{8,0},{12,4},{16,24},{20,28},{24,16},{28,20},{1,9},{5... | collective-permute-start | bytes 1179656 | tf_op jit(solution)/shard_map/ppermute | solution.py:530
  449.0 36.8 %collective-permute-start.51 = (bf16[1024,1024]{1,0:T(8,128)(2,1)S(1)}, bf16[1024,1024]{1,0:T(8,128)(2,1)S(1)}, u32[]{:S(2)}, u32[]{:S(2)}) collective-permute-start(bf16[1024,1024]{1,0:T(8,128)(2,1)S(1)} %copy-done.21), channel_id=1, source_target_pairs={{0,1},{1,0},{2,3},{3,2},{4,5},{5,4},{6,7},{7,6},{8,9},{9,8},{10,11... | collective-permute-start | bytes 6291464 | tf_op jit(solution)/shard_map/ppermute | solution.py:530
  449.7 9.4 %collective-permute-start.50 = (bf16[256,1,128]{2,0,1:T(8,128)(2,1)S(1)}, bf16[256,1,128]{2,0,1:T(8,128)(2,1)S(1)}, u32[]{:S(2)}, u32[]{:S(2)}) collective-permute-start(bf16[256,1,128]{2,0,1:T(8,128)(2,1)S(1)} %constant_dynamic-slice_fusion.4), channel_id=1, source_target_pairs={{0,16},{4,20},{8,24},{12,28},{16,0},{20,4},{24,8},{28,12},{1,17},{... | collective-permute-start | bytes 196616 | tf_op jit(solution)/shard_map/ppermute | solution.py:530
  457.9 21.1 %collective-permute-start.21 = (bf16[2,8,32,1024]{3,2,1,0:T(8,128)(2,1)S(1)}, bf16[2,8,32,1024]{3,2,1,0:T(8,128)(2,1)S(1)}, u32[]{:S(2)}, u32[]{:S(2)}) collective-permute-start(bf16[2,8,32,1024]{3,2,1,0:T(8,128)(2,1)S(1)} %get-tuple-element.115), channel_id=1, source_target_pairs={{0,2},{1,3},{2,0},{3,1},{4,6},{5,7},{6,4},{7,5},{8,10},{9,11},{10,... | collective-permute-start | bytes 3145736 | tf_op jit(solution)/shard_map/ppermute | solution.py:530
  459.1 8.7 %collective-permute-start.35 = (bf16[3,1,128,256]{3,2,1,0:T(8,128)(2,1)S(1)}, bf16[3,1,128,256]{3,2,1,0:T(8,128)(2,1)S(1)}, u32[]{:S(2)}, u32[]{:S(2)}) collective-permute-start(bf16[3,1,128,256]{3,2,1,0:T(8,128)(2,1)S(1)} %constant_dynamic-slice_fusion.11), channel_id=1, source_target_pairs={{0,16},{4,20},{8,24},{12,28},{16,0},{20,4},{24,8},{28,12},{1,17},{... | collective-permute-start | bytes 589832 | tf_op jit(solution)/shard_map/ppermute | solution.py:530
  467.9 21.6 %collective-permute-start.55 = (bf16[1024,1024]{1,0:T(8,128)(2,1)S(1)}, bf16[1024,1024]{1,0:T(8,128)(2,1)S(1)}, u32[]{:S(2)}, u32[]{:S(2)}) collective-permute-start(bf16[1024,1024]{1,0:T(8,128)(2,1)S(1)} %copy-done.20), channel_id=1, source_target_pairs={{0,1},{1,0},{2,3},{3,2},{4,5},{5,4},{6,7},{7,6},{8,9},{9,8},{10,11... | collective-permute-start | bytes 6291464 | tf_op jit(solution)/shard_map/ppermute | solution.py:530
  468.7 47.0 %collective-permute-start.23 = (bf16[8,32,1024]{2,1,0:T(8,128)(2,1)}, bf16[8,32,1024]{2,1,0:T(8,128)(2,1)}, u32[]{:S(2)}, u32[]{:S(2)}) collective-permute-start(bf16[8,32,1024]{2,1,0:T(8,128)(2,1)} %bitcast.73), channel_id=1, source_target_pairs={{0,4},{4,0},{8,12},{12,8},{16,20},{20,16},{24,28},{28,24},{1,5},{5... | collective-permute-start | bytes 1572872 | tf_op jit(solution)/shard_map/ppermute | solution.py:530
  479.0 22.3 %collective-permute-start.42 = (bf16[3,1024,256]{2,1,0:T(8,128)(2,1)}, bf16[3,1024,256]{2,1,0:T(8,128)(2,1)}, u32[]{:S(2)}, u32[]{:S(2)}) collective-permute-start(bf16[3,1024,256]{2,1,0:T(8,128)(2,1)} %slice_bitcast_fusion.2), channel_id=1, source_target_pairs={{0,1},{1,0},{2,3},{3,2},{4,5},{5,4},{6,7},{7,6},{8,9},{9,8},{10,11... | collective-permute-start | bytes 4718600 | tf_op jit(solution)/shard_map/ppermute | solution.py:530
  481.3 117.3 %collective-permute-start.22 = (bf16[2,2,8,32,1024]{4,3,2,1,0:T(8,128)(2,1)}, bf16[2,2,8,32,1024]{4,3,2,1,0:T(8,128)(2,1)}, u32[]{:S(2)}, u32[]{:S(2)}) collective-permute-start(bf16[2,2,8,32,1024]{4,3,2,1,0:T(8,128)(2,1)} %get-tuple-element.103), channel_id=1, source_target_pairs={{0,1},{1,0},{2,3},{3,2},{4,5},{5,4},{6,7},{7,6},{8,9},{9,8},{10,11... | collective-permute-start | bytes 6291464 | tf_op jit(solution)/shard_map/ppermute | solution.py:530
  486.2 25.4 %collective-permute-start.25 = (bf16[8,2,32,1024]{3,2,0,1:T(8,128)(2,1)}, bf16[8,2,32,1024]{3,2,0,1:T(8,128)(2,1)}, u32[]{:S(2)}, u32[]{:S(2)}) collective-permute-start(bf16[8,2,32,1024]{3,2,0,1:T(8,128)(2,1)} %dynamic-slice_bitcast_fusion.1), channel_id=1, source_target_pairs={{0,2},{1,3},{2,0},{3,1},{4,6},{5,7},{6,4},{7,5},{8,10},{9,11},{10,... | collective-permute-start | bytes 3145736 | tf_op jit(solution)/shard_map/ppermute | solution.py:530
  489.4 31.0 %collective-permute-start.52 = (bf16[4,128,1024]{2,1,0:T(8,128)(2,1)}, bf16[4,128,1024]{2,1,0:T(8,128)(2,1)}, u32[]{:S(2)}, u32[]{:S(2)}) collective-permute-start(bf16[4,128,1024]{2,1,0:T(8,128)(2,1)} %dynamic-slice_bitcast_fusion), channel_id=1, source_target_pairs={{0,4},{4,0},{8,12},{12,8},{16,20},{20,16},{24,28},{28,24},{1,5},{5... | collective-permute-start | bytes 3145736 | tf_op jit(solution)/shard_map/ppermute | solution.py:530
  501.3 55.2 %collective-permute-start.56 = (bf16[1024,4,128]{2,0,1:T(8,128)(2,1)S(1)}, bf16[1024,4,128]{2,0,1:T(8,128)(2,1)S(1)}, u32[]{:S(2)}, u32[]{:S(2)}) collective-permute-start(bf16[1024,4,128]{2,0,1:T(8,128)(2,1)S(1)} %bitcast.344), channel_id=1, source_target_pairs={{0,4},{4,0},{8,12},{12,8},{16,20},{20,16},{24,28},{28,24},{1,5},{5... | collective-permute-start | bytes 3145736 | tf_op jit(solution)/shard_map/ppermute | solution.py:530
  511.6 84.1 %collective-permute-start.43 = (bf16[3,4,128,256]{3,2,1,0:T(8,128)(2,1)S(1)}, bf16[3,4,128,256]{3,2,1,0:T(8,128)(2,1)S(1)}, u32[]{:S(2)}, u32[]{:S(2)}) collective-permute-start(bf16[3,4,128,256]{3,2,1,0:T(8,128)(2,1)S(1)} %dynamic-slice_bitcast_fusion.2), channel_id=1, source_target_pairs={{0,4},{4,0},{8,12},{12,8},{16,20},{20,16},{24,28},{28,24},{1,5},{5... | collective-permute-start | bytes 2359304 | tf_op jit(solution)/shard_map/ppermute | solution.py:530
  517.9 1.3 collective-permute-start.28
  519.3 59.0 %collective-permute-start.26 = (bf16[2,8,32,1024]{3,2,1,0:T(8,128)(2,1)S(1)}, bf16[2,8,32,1024]{3,2,1,0:T(8,128)(2,1)S(1)}, u32[]{:S(2)}, u32[]{:S(2)}) collective-permute-start(bf16[2,8,32,1024]{3,2,1,0:T(8,128)(2,1)S(1)} %get-tuple-element.101), channel_id=1, source_target_pairs={{0,2},{1,3},{2,0},{3,1},{4,6},{5,7},{6,4},{7,5},{8,10},{9,11},{10,... | collective-permute-start | bytes 3145736 | tf_op jit(solution)/shard_map/ppermute | solution.py:530
  520.4 25.5 %collective-permute-start.29 = (f32[11,1024]{1,0:T(8,128)S(1)}, f32[11,1024]{1,0:T(8,128)S(1)}, u32[]{:S(2)}, u32[]{:S(2)}) collective-permute-start(f32[11,1024]{1,0:T(8,128)S(1)} %fusion.57), channel_id=1, source_target_pairs={{0,2},{1,3},{2,0},{3,1},{4,6},{5,7},{6,4},{7,5},{8,10},{9,11},{10,... | collective-permute-start | bytes 135176 | tf_op jit(solution)/shard_map/ppermute | solution.py:530
  545.9 9.3 %collective-permute-start.30 = (f32[11,1024]{1,0:T(8,128)S(1)}, f32[11,1024]{1,0:T(8,128)S(1)}, u32[]{:S(2)}, u32[]{:S(2)}) collective-permute-start(f32[11,1024]{1,0:T(8,128)S(1)} %add.415), channel_id=1, source_target_pairs={{0,4},{4,0},{8,12},{12,8},{16,20},{20,16},{24,28},{28,24},{1,5},{5... | collective-permute-start | bytes 135176 | tf_op jit(solution)/shard_map/ppermute | solution.py:530
  555.2 22.9 %collective-permute-start.53 = (bf16[2,128,1024]{2,1,0:T(8,128)(2,1)S(1)}, bf16[2,128,1024]{2,1,0:T(8,128)(2,1)S(1)}, u32[]{:S(2)}, u32[]{:S(2)}) collective-permute-start(bf16[2,128,1024]{2,1,0:T(8,128)(2,1)S(1)} %dynamic-slice_bitcast_fusion.5), channel_id=1, source_target_pairs={{0,8},{4,12},{8,0},{12,4},{16,24},{20,28},{24,16},{28,20},{1,9},{5... | collective-permute-start | bytes 1572872 | tf_op jit(solution)/shard_map/ppermute | solution.py:530
  556.5 12.8 %collective-permute-start.31 = (f32[11,1024]{1,0:T(8,128)S(1)}, f32[11,1024]{1,0:T(8,128)S(1)}, u32[]{:S(2)}, u32[]{:S(2)}) collective-permute-start(f32[11,1024]{1,0:T(8,128)S(1)} %add.416), channel_id=1, source_target_pairs={{0,8},{4,12},{8,0},{12,4},{16,24},{20,28},{24,16},{28,20},{1,9},{5... | collective-permute-start | bytes 135176 | tf_op jit(solution)/shard_map/ppermute | solution.py:530
  569.3 5.9 collective-permute-start.32
  575.1 15.3 %collective-permute-start.57 = (bf16[1024,2,128]{2,0,1:T(8,128)(2,1)S(1)}, bf16[1024,2,128]{2,0,1:T(8,128)(2,1)S(1)}, u32[]{:S(2)}, u32[]{:S(2)}) collective-permute-start(bf16[1024,2,128]{2,0,1:T(8,128)(2,1)S(1)} %dynamic-slice_bitcast_fusion.4), channel_id=1, source_target_pairs={{0,8},{4,12},{8,0},{12,4},{16,24},{20,28},{24,16},{28,20},{1,9},{5... | collective-permute-start | bytes 1572872 | tf_op jit(solution)/shard_map/ppermute | solution.py:530
  578.6 42.2 %collective-permute-start.27 = (bf16[2,2,8,32,1024]{4,3,2,1,0:T(8,128)(2,1)S(1)}, bf16[2,2,8,32,1024]{4,3,2,1,0:T(8,128)(2,1)}, u32[]{:S(2)}, u32[]{:S(2)}) collective-permute-start(bf16[2,2,8,32,1024]{4,3,2,1,0:T(8,128)(2,1)S(1)} %get-tuple-element.99), channel_id=1, source_target_pairs={{0,1},{1,0},{2,3},{3,2},{4,5},{5,4},{6,7},{7,6},{8,9},{9,8},{10,11... | collective-permute-start | bytes 6291464 | tf_op jit(solution)/shard_map/ppermute | solution.py:530
  578.7 31.2 %collective-permute-start.54 = (bf16[1,128,1024]{2,1,0:T(8,128)(2,1)S(1)}, bf16[1,128,1024]{2,1,0:T(8,128)(2,1)}, u32[]{:S(2)}, u32[]{:S(2)}) collective-permute-start(bf16[1,128,1024]{2,1,0:T(8,128)(2,1)S(1)} %constant_dynamic-slice_fusion.3), channel_id=1, source_target_pairs={{0,16},{4,20},{8,24},{12,28},{16,0},{20,4},{24,8},{28,12},{1,17},{... | collective-permute-start | bytes 786440 | tf_op jit(solution)/shard_map/ppermute | solution.py:530
  590.7 21.2 %collective-permute-start.58 = (bf16[1024,1,128]{2,0,1:T(8,128)(2,1)S(1)}, bf16[1024,1,128]{2,0,1:T(8,128)(2,1)}, u32[]{:S(2)}, u32[]{:S(2)}) collective-permute-start(bf16[1024,1,128]{2,0,1:T(8,128)(2,1)S(1)} %constant_dynamic-slice_fusion), channel_id=1, source_target_pairs={{0,16},{4,20},{8,24},{12,28},{16,0},{20,4},{24,8},{28,12},{1,17},{... | collective-permute-start | bytes 786440 | tf_op jit(solution)/shard_map/ppermute | solution.py:530
  596.0 15.7 %collective-permute-start.44 = (bf16[3,2,128,256]{3,2,1,0:T(8,128)(2,1)S(1)}, bf16[3,2,128,256]{3,2,1,0:T(8,128)(2,1)S(1)}, u32[]{:S(2)}, u32[]{:S(2)}) collective-permute-start(bf16[3,2,128,256]{3,2,1,0:T(8,128)(2,1)S(1)} %dynamic-slice_bitcast_fusion.10), channel_id=1, source_target_pairs={{0,8},{4,12},{8,0},{12,4},{16,24},{20,28},{24,16},{28,20},{1,9},{5... | collective-permute-start | bytes 1179656 | tf_op jit(solution)/shard_map/ppermute | solution.py:530
  611.8 8.2 %collective-permute-start.45 = (bf16[3,1,128,256]{3,2,1,0:T(8,128)(2,1)S(1)}, bf16[3,1,128,256]{3,2,1,0:T(8,128)(2,1)S(1)}, u32[]{:S(2)}, u32[]{:S(2)}) collective-permute-start(bf16[3,1,128,256]{3,2,1,0:T(8,128)(2,1)S(1)} %constant_dynamic-slice_fusion.7), channel_id=1, source_target_pairs={{0,16},{4,20},{8,24},{12,28},{16,0},{20,4},{24,8},{28,12},{1,17},{... | collective-permute-start | bytes 589832 | tf_op jit(solution)/shard_map/ppermute | solution.py:530
  (37 other events, 181.4 us)
